TPU v7x, 512 devices: a whole 4x8x8 slice. The times are simulated.
512 devices in a mesh: grid: 64 (over x, z, core), mem: 8 (over y).
Axes of the slice: x: 4, y: 8, z: 8, core: 2. Of those that a mesh axis runs over, the one named last changes fastest.
Arguments:
- ens: bfloat16 [80, 4, 32, 65536], P('mem', None, None, 'grid'), may hold values from -6 to 6
- control: float32 [4, 32, 65536], P(None, None, 'grid'), may hold values from -6 to 6
- col_count: int32 [512], P('grid'), may hold values from 64 to 128, as said below
- level_index: int32 [32], replicated, may hold values from 43 to 136, as said below
- pair_blocks: int32 [6144, 2], P('grid'), may hold values from 0 to 511, as said below
- loc_blocks: bfloat16 [6144, 128, 128], P('grid'), may hold values from -0.109375 to 0.109375
Outputs:
- mixed: float32 [4, 32, 65536], P(None, None, ('grid', 'mem'))
Inputs may be any that keep to these rules, and one draw needn't show every extreme that they name: `pair_blocks`: rows come in groups of 12, one group for each block b in order; group b holds the pairs (b, (b + k) mod 512) for k = 0, k = 12 and 10 further distinct k between 1 and 11. `col_count`: some block is full. `level_index`: strictly increasing by steps of 1 to 3; the last is 136.
All inputs are finite; a program needn't handle non-finite values.
Results may differ from a plain program's by a relative error of at most 0.0029.
Values may be sent and summed in bfloat16 or wider, within the bound.
No kernel may reach another device: no remote copies, remote signals or barrier semaphores. Data moves between devices by JAX's collectives and lax.ppermute only.
A program may use at most 64 MiB of HBM per device.

v0:
```python
import jax
import jax.numpy as jnp
from jax import lax
from jax.sharding import PartitionSpec as P

SPAN = 12


vertical_scale = 8.0


def passed_along(array, axis, by):
    peers = lax.axis_size(axis)
    return lax.ppermute(array, axis, [(i, (i + by) % peers) for i in range(peers)])


def per_device(ens, control, col_count, level_index, pair_blocks, loc_blocks):
    blocks_dev = col_count.shape[0]
    width = loc_blocks.shape[1]
    per_block = pair_blocks.shape[0] // blocks_dev
    reach = (blocks_dev - 1 + SPAN) // blocks_dev
    devices = lax.axis_size("grid")
    here = lax.axis_index("grid")
    members_dev = ens.shape[0]
    slot_count = ens.shape[1]
    level_count = ens.shape[2]
    columns = jnp.arange(blocks_dev * width)
    live = (columns % width < jnp.repeat(col_count, width)).astype(jnp.float32)
    masked = control * live
    levels = level_index.astype(jnp.float32)
    vert = jnp.exp(-jnp.abs(levels[:, None] - levels[None, :]) / vertical_scale)
    weighted = jnp.sum(ens.astype(jnp.float32) * masked[None], axis=1)
    lifted = jnp.einsum("kl,mlc->mkc", vert, weighted, precision=lax.Precision.HIGHEST).astype(
        jnp.bfloat16
    )
    own = lifted.reshape(members_dev, level_count, blocks_dev, width).transpose(2, 0, 1, 3)
    ens_blocks = ens.reshape(members_dev, slot_count, level_count, blocks_dev, width)
    fetched = [own]
    for offset in range(1, reach + 1):
        fetched.append(passed_along(own, "grid", -offset))
    table = jnp.concatenate(fetched, axis=0)
    far_count = (reach + 1) * blocks_dev
    first = pair_blocks[:, 0]
    second = pair_blocks[:, 1]
    near_index = first - here * blocks_dev
    distance = jnp.mod(second // blocks_dev - here, devices)
    far_index = distance * blocks_dev + second % blocks_dev

    def pair_group(carry, item):
        near_acc, far_acc = carry
        group_id, near_idx, far_idx, local_loc = item
        near_rows = own[group_id]
        far_rows = table[far_idx]
        to_near = jnp.einsum(
            "pab,pmlb->mla", local_loc, far_rows, preferred_element_type=jnp.float32
        )
        apart = (far_idx != near_idx).astype(jnp.float32)
        to_far = jnp.einsum(
            "pab,mla->pmlb", local_loc, near_rows, preferred_element_type=jnp.float32
        )
        to_far = to_far * apart[:, None, None, None]
        near_acc = near_acc.at[group_id].add(to_near)
        far_acc = far_acc.at[far_idx].add(to_far)
        return ((near_acc, far_acc), None)

    near_start = jnp.zeros((blocks_dev, members_dev, level_count, width), jnp.float32)
    far_start = jnp.zeros((far_count, members_dev, level_count, width), jnp.float32)
    items = (
        jnp.arange(blocks_dev, dtype=jnp.int32),
        near_index.reshape(blocks_dev, per_block),
        far_index.reshape(blocks_dev, per_block),
        loc_blocks.reshape(blocks_dev, per_block, width, width),
    )
    (near_acc, far_acc), unused = lax.scan(pair_group, (near_start, far_start), items)
    far_parts = far_acc.reshape(reach + 1, blocks_dev, members_dev, level_count, width)
    spread = near_acc + far_parts[0]
    for offset in range(1, reach + 1):
        spread = spread + passed_along(far_parts[offset], "grid", offset)
    summed = jnp.sum(ens_blocks.astype(jnp.float32) * spread.transpose(1, 2, 0, 3)[:, None], axis=0)
    members_all = members_dev * lax.axis_size("mem")
    terms = summed.reshape(slot_count, level_count, blocks_dev * width) * live / (members_all - 1)
    return lax.psum_scatter(terms, "mem", scatter_dimension=2, tiled=True)


def solution(mesh):
    return jax.shard_map(
        per_device,
        mesh=mesh,
        in_specs=(
            P("mem", None, None, "grid"),
            P(None, None, "grid"),
            P("grid"),
            P(),
            P("grid", None),
            P("grid", None, None),
        ),
        out_specs=P(None, None, ("grid", "mem")),
        check_vma=False,
    )
```

profile of v0, /device:TPU:6, one launch (start us, length us, event | category | flops | bytes accessed | tf_op | source)
XLA Modules:
  0.0 260.6 jit_solution(15496828980445087857)
XLA Ops:
  9.0 2.5 fusion.13
  11.6 1.3 fusion.15
  13.8 11.2 %collective-permute-start.1 = (bf16[8,10,32,128]{3,2,1,0:T(8,128)(2,1)}, bf16[8,10,32,128]{3,2,1,0:T(8,128)(2,1)S(1)}, u32[]{:S(2)}, u32[]{:S(2)}) collective-permute-start(bf16[8,10,32,128]{3,2,1,0:T(8,128)(2,1)} %bitcast.57), channel_id=1, source_target_pairs={{0,496},{8,504},{16,0},{24,8},{32,16},{40,24},{48,32},{56,40},{64,... | collective-permute-start | bytes 1966088 | tf_op jit(solution)/shard_map/ppermute | solution.py:14
  25.0 1.9 collective-permute-start
  27.2 12.1 %collective-permute-done.1 = bf16[8,10,32,128]{3,2,1,0:T(8,128)(2,1)S(1)} collective-permute-done((bf16[8,10,32,128]{3,2,1,0:T(8,128)(2,1)}, bf16[8,10,32,128]{3,2,1,0:T(8,128)(2,1)S(1)}, u32[]{:S(2)}, u32[]{:S(2)}) %collective-permute-start.1) | collective-permute-done | bytes 655392 | tf_op jit(solution)/shard_map/ppermute | solution.py:14
  39.3 7.0 %collective-permute-done = bf16[8,10,32,128]{3,2,1,0:T(8,128)(2,1)S(1)} collective-permute-done((bf16[8,10,32,128]{3,2,1,0:T(8,128)(2,1)}, bf16[8,10,32,128]{3,2,1,0:T(8,128)(2,1)S(1)}, u32[]{:S(2)}, u32[]{:S(2)}) %collective-permute-start) | collective-permute-done | bytes 655392 | tf_op jit(solution)/shard_map/ppermute | solution.py:14
  46.3 2.6 pad_maximum_fusion
  49.1 2.4 broadcast_in_dim.7
  51.5 111.4 %while.13 = (s32[]{:T(128)}, f32[8,10,32,128]{3,2,1,0:T(8,128)S(1)}, f32[24,10,32,128]{3,2,1,0:T(8,128)}, s32[8]{0:T(128)S(1)}, s32[8,12]{1,0:T(8,128)S(1)}, /*i...) while((s32[]{:T(128)}, ...), condition=%wide.region_4.5_spmd, body=%wide.region_1.4_spmd.sunk | while | flops 252724320 | bytes 15947924 | solution.py:74
  54.8 2.3 gather_fusion
  57.1 2.0 fusion.51
  59.1 1.5 multiply_bitcast_fusion.2
  60.8 4.6 %scatter_fusion = f32[24,10,32,128]{3,2,1,0:T(8,128)} fusion(f32[24,10,32,128]{3,2,1,0:T(8,128)} %get-tuple-element.160, s32[12]{0:T(128)S(1)} %fusion.50, f32[12,10,32,128]{3,2,1,0:T(8,128)S(1)} %copy.23), kind=kCustom, calls=%fused_computation.1.clone.1 | custom fusion | flops 491520 | bytes 5898288 | tf_op jit(solution)/shard_map/while/body/eval_jaxpr/scatter-add | solution.py:63
  68.7 2.3 gather_fusion
  71.0 2.0 fusion.51
  73.1 1.4 multiply_bitcast_fusion.2
  74.7 4.6 %scatter_fusion = f32[24,10,32,128]{3,2,1,0:T(8,128)} fusion(f32[24,10,32,128]{3,2,1,0:T(8,128)} %get-tuple-element.160, s32[12]{0:T(128)S(1)} %fusion.50, f32[12,10,32,128]{3,2,1,0:T(8,128)S(1)} %copy.23), kind=kCustom, calls=%fused_computation.1.clone.1 | custom fusion | flops 491520 | bytes 5898288 | tf_op jit(solution)/shard_map/while/body/eval_jaxpr/scatter-add | solution.py:63
  82.6 2.3 gather_fusion
  84.9 2.0 fusion.51
  87.0 1.5 multiply_bitcast_fusion.2
  88.6 4.6 %scatter_fusion = f32[24,10,32,128]{3,2,1,0:T(8,128)} fusion(f32[24,10,32,128]{3,2,1,0:T(8,128)} %get-tuple-element.160, s32[12]{0:T(128)S(1)} %fusion.50, f32[12,10,32,128]{3,2,1,0:T(8,128)S(1)} %copy.23), kind=kCustom, calls=%fused_computation.1.clone.1 | custom fusion | flops 491520 | bytes 5898288 | tf_op jit(solution)/shard_map/while/body/eval_jaxpr/scatter-add | solution.py:63
  96.5 2.3 gather_fusion
  98.8 2.0 fusion.51
  100.9 1.4 multiply_bitcast_fusion.2
  102.5 4.6 %scatter_fusion = f32[24,10,32,128]{3,2,1,0:T(8,128)} fusion(f32[24,10,32,128]{3,2,1,0:T(8,128)} %get-tuple-element.160, s32[12]{0:T(128)S(1)} %fusion.50, f32[12,10,32,128]{3,2,1,0:T(8,128)S(1)} %copy.23), kind=kCustom, calls=%fused_computation.1.clone.1 | custom fusion | flops 491520 | bytes 5898288 | tf_op jit(solution)/shard_map/while/body/eval_jaxpr/scatter-add | solution.py:63
  110.5 2.3 gather_fusion
  112.8 2.0 fusion.51
  114.8 1.5 multiply_bitcast_fusion.2
  116.5 4.7 %scatter_fusion = f32[24,10,32,128]{3,2,1,0:T(8,128)} fusion(f32[24,10,32,128]{3,2,1,0:T(8,128)} %get-tuple-element.160, s32[12]{0:T(128)S(1)} %fusion.50, f32[12,10,32,128]{3,2,1,0:T(8,128)S(1)} %copy.23), kind=kCustom, calls=%fused_computation.1.clone.1 | custom fusion | flops 491520 | bytes 5898288 | tf_op jit(solution)/shard_map/while/body/eval_jaxpr/scatter-add | solution.py:63
  124.4 2.3 gather_fusion
  126.7 2.0 fusion.51
  128.8 1.5 multiply_bitcast_fusion.2
  130.4 4.6 %scatter_fusion = f32[24,10,32,128]{3,2,1,0:T(8,128)} fusion(f32[24,10,32,128]{3,2,1,0:T(8,128)} %get-tuple-element.160, s32[12]{0:T(128)S(1)} %fusion.50, f32[12,10,32,128]{3,2,1,0:T(8,128)S(1)} %copy.23), kind=kCustom, calls=%fused_computation.1.clone.1 | custom fusion | flops 491520 | bytes 5898288 | tf_op jit(solution)/shard_map/while/body/eval_jaxpr/scatter-add | solution.py:63
  138.4 2.3 gather_fusion
  140.7 2.0 fusion.51
  142.7 1.4 multiply_bitcast_fusion.2
  144.4 4.6 %scatter_fusion = f32[24,10,32,128]{3,2,1,0:T(8,128)} fusion(f32[24,10,32,128]{3,2,1,0:T(8,128)} %get-tuple-element.160, s32[12]{0:T(128)S(1)} %fusion.50, f32[12,10,32,128]{3,2,1,0:T(8,128)S(1)} %copy.23), kind=kCustom, calls=%fused_computation.1.clone.1 | custom fusion | flops 491520 | bytes 5898288 | tf_op jit(solution)/shard_map/while/body/eval_jaxpr/scatter-add | solution.py:63
  152.3 2.3 gather_fusion
  154.6 2.0 fusion.51
  156.6 1.5 multiply_bitcast_fusion.2
  158.3 4.6 %scatter_fusion = f32[24,10,32,128]{3,2,1,0:T(8,128)} fusion(f32[24,10,32,128]{3,2,1,0:T(8,128)} %get-tuple-element.160, s32[12]{0:T(128)S(1)} %fusion.50, f32[12,10,32,128]{3,2,1,0:T(8,128)S(1)} %copy.23), kind=kCustom, calls=%fused_computation.1.clone.1 | custom fusion | flops 491520 | bytes 5898288 | tf_op jit(solution)/shard_map/while/body/eval_jaxpr/scatter-add | solution.py:63
  162.9 1.9 fusion.36
  164.9 1.9 collective-permute-start.2
  166.8 1.9 collective-permute-start.3
  168.7 28.7 %collective-permute-done.2 = f32[8,10,32,128]{3,2,1,0:T(8,128)S(1)} collective-permute-done((f32[8,10,32,128]{3,2,1,0:T(8,128)S(1)}, f32[8,10,32,128]{3,2,1,0:T(8,128)S(1)}, u32[]{:S(2)}, u32[]{:S(2)}) %collective-permute-start.2) | collective-permute-done | bytes 1310752 | tf_op jit(solution)/shard_map/ppermute | solution.py:14
  197.4 5.3 %collective-permute-done.3 = f32[8,10,32,128]{3,2,1,0:T(8,128)S(1)} collective-permute-done((f32[8,10,32,128]{3,2,1,0:T(8,128)S(1)}, f32[8,10,32,128]{3,2,1,0:T(8,128)S(1)}, u32[]{:S(2)}, u32[]{:S(2)}) %collective-permute-start.3) | collective-permute-done | bytes 1310752 | tf_op jit(solution)/shard_map/ppermute | solution.py:14
  202.7 1.8 copy_bitcast_fusion
  206.4 47.4 %reduce-scatter.2.cloned.1.call-done = f32[4,32,128]{2,1,0:T(8,128)} async-done(((f32[4,32,1024]{2,1,0:T(8,128)}), f32[4,32,128]{2,1,0:T(8,128)}) %reduce-scatter.2.cloned.1.call-update) | async-done | bytes 65552 | tf_op jit(solution)/shard_map/reduce_scatter | solution.py:82
  (68 shorter events, 18.6 us)
Async XLA Ops:
  6.5 247.2 %reduce-scatter.2.cloned.1.call-start = ((), (), s32[]{:S(2)}) async-start(), calls=%async_computation.1 | async-start | bytes 589824 | tf_op jit(solution)/shard_map/reduce_scatter | solution.py:82
  11.6 15.4 %copy-start.2 = (s32[96,2]{0,1:T(2,128)S(1)}, s32[96,2]{0,1:T(2,128)}, u32[]{:S(2)}) copy-start(s32[96,2]{0,1:T(2,128)} %param.14) | copy-start | bytes 2308
  13.8 25.5 %collective-permute-start.1 = (bf16[8,10,32,128]{3,2,1,0:T(8,128)(2,1)}, bf16[8,10,32,128]{3,2,1,0:T(8,128)(2,1)S(1)}, u32[]{:S(2)}, u32[]{:S(2)}) collective-permute-start(bf16[8,10,32,128]{3,2,1,0:T(8,128)(2,1)} %bitcast.57), channel_id=1, source_target_pairs={{0,496},{8,504},{16,0},{24,8},{32,16},{40,24},{48,32},{56,40},{64,... | collective-permute-start | bytes 1966088 | tf_op jit(solution)/shard_map/ppermute | solution.py:14
  25.0 21.3 %collective-permute-start = (bf16[8,10,32,128]{3,2,1,0:T(8,128)(2,1)}, bf16[8,10,32,128]{3,2,1,0:T(8,128)(2,1)S(1)}, u32[]{:S(2)}, u32[]{:S(2)}) collective-permute-start(bf16[8,10,32,128]{3,2,1,0:T(8,128)(2,1)} %bitcast.57), channel_id=1, source_target_pairs={{0,504},{8,0},{16,8},{24,16},{32,24},{40,32},{48,40},{56,48},{64,5... | collective-permute-start | bytes 1966088 | tf_op jit(solution)/shard_map/ppermute | solution.py:14
  49.1 2.4 copy-start.1
  164.9 32.5 %collective-permute-start.2 = (f32[8,10,32,128]{3,2,1,0:T(8,128)S(1)}, f32[8,10,32,128]{3,2,1,0:T(8,128)S(1)}, u32[]{:S(2)}, u32[]{:S(2)}) collective-permute-start(f32[8,10,32,128]{3,2,1,0:T(8,128)S(1)} %get-tuple-element.87), channel_id=1, source_target_pairs={{0,8},{8,16},{16,24},{24,32},{32,40},{40,48},{48,56},{56,64},{64,7... | collective-permute-start | bytes 3932168 | tf_op jit(solution)/shard_map/ppermute | solution.py:14
  166.8 35.9 %collective-permute-start.3 = (f32[8,10,32,128]{3,2,1,0:T(8,128)S(1)}, f32[8,10,32,128]{3,2,1,0:T(8,128)S(1)}, u32[]{:S(2)}, u32[]{:S(2)}) collective-permute-start(f32[8,10,32,128]{3,2,1,0:T(8,128)S(1)} %get-tuple-element.88), channel_id=1, source_target_pairs={{0,16},{8,24},{16,32},{24,40},{32,48},{40,56},{48,64},{56,72},{64,... | collective-permute-start | bytes 3932168 | tf_op jit(solution)/shard_map/ppermute | solution.py:14
  202.7 2.1 copy-start
Sparse Core Ops, SparseCore 0:
  206.5 47.2 reduce-scatter.1
where the time goes:
time: 262 us; the launch traced here: 261 us
  waiting for transfers between devices  101 us (39%)
  other arithmetic  54.3 us (21%)
  local copies, waits for them, and re-layouts  30.8 us (12%)
  matrix products  29.2 us (11%)
  starting transfers between devices  17 us (6%)
  loops' own time  15.2 us (6%)
  between operations  13.5 us (5%)
    ppermute x4, waiting for transfers between devices, passed_along(): lax.ppermute(array, axis, [(i, (i + by) % peers) for i in range(peers)])  53.2 us
    reduce_scatter x1, waiting for transfers between devices, per_device(): return lax.psum_scatter(terms, 'mem', scatter_dimension=2, tiled=True)  47.4 us
    scatter-add x8, other arithmetic, pair_group(): far_acc = far_acc.at[far_idx].add(to_far)  37 us
    gather x8, local copies, waits for them, and re-layouts, pair_group(): far_rows = table[far_idx]  18.2 us
    ppermute x4, starting transfers between devices, passed_along(): lax.ppermute(array, axis, [(i, (i + by) % peers) for i in range(peers)])  17 us
    dot_general x8, matrix products, pair_group(): jnp.einsum('pab,pmlb->mla', local_loc, far_rows, preferred_element_type=j...  16.3 us
    another operation x1, loops' own time, per_device(): lax.scan(pair_group, (near_start, far_start), items)  15.2 us
    dot_general x8, matrix products, pair_group(): jnp.einsum('pab,mla->pmlb', local_loc, near_rows, preferred_element_type=...  11.6 us
  transfers between devices with their start and end apart: 5, of which 5 were waited for; matrix products, arithmetic and copies ran while one was open for 0% of the time, Pallas kernels for 0%

commit v1 on v0

v1 whole, which is shorter than its diff:
```python
import functools

import jax
import jax.numpy as jnp
from jax import lax
from jax.experimental import pallas as pl
from jax.experimental.pallas import tpu as pltpu
from jax.sharding import PartitionSpec as P

SPAN = 12
WIDTH = 128
DEV = 8
TWO = 2 * WIDTH
LANES = 16 * WIDTH

vertical_scale = 8.0

F32 = jnp.float32
BF16 = jnp.bfloat16
SMEM = pl.BlockSpec(memory_space=pltpu.SMEM)


def dot(a, b):
    return lax.dot_general(a, b, (((1,), (0,)), ((), ())), preferred_element_type=F32)


def dot_t(a, b):
    return lax.dot_general(a, b, (((1,), (1,)), ((), ())), preferred_element_type=F32)


def is_odd(pairs_ref):
    return lax.rem(pairs_ref[0, 0] // DEV, 2) == 1


def fill_band(pairs_ref, loc_ref, g, per, blocks, store):
    zero = jnp.zeros((WIDTH, WIDTH), BF16)
    store(0, SPAN + 1, zero)
    store(1, 0, zero)
    for ii in range(2):
        left = SPAN * (SPAN + 1) // 2
        for p in range(per):
            at = (2 * g + ii) * per + p
            k = pairs_ref[1, at] - pairs_ref[0, at]
            k = jnp.where(k < 0, k + blocks, k)
            left = left - k
            store(ii, k + ii, loc_ref[ii * per + p])
        store(ii, left + ii, zero)


def lift_kernel(members, slots, levels, per, blocks, pairs_ref, count_ref, level_ref, ens_ref, control_ref, loc_ref,
                own_ref, pay1_ref, pay3_ref, mrg_ref, lifted, band, vert):
    g = pl.program_id(0)
    odd = is_odd(pairs_ref)
    group = WIDTH // levels

    @pl.when(g == 0)
    def _():
        lane = lax.broadcasted_iota(jnp.int32, (levels, WIDTH), 1)
        row = lax.broadcasted_iota(jnp.int32, (levels, WIDTH), 0)
        by_lane = jnp.zeros((levels, WIDTH), F32)
        by_row = jnp.zeros((levels, WIDTH), F32)
        for l in range(levels):
            value = level_ref[l].astype(F32)
            by_lane = jnp.where(lane % levels == l, value, by_lane)
            by_row = jnp.where(row == l, value, by_row)
        v = jnp.exp(-jnp.abs(by_row - by_lane) / vertical_scale)
        for q in range(group):
            part = jnp.where(lane // levels == q, v, 0.0)
            high = part.astype(BF16)
            vert[0, q * levels:(q + 1) * levels, :] = high
            vert[1, q * levels:(q + 1) * levels, :] = (part - high.astype(F32)).astype(BF16)

    lane = lax.broadcasted_iota(jnp.int32, (levels, TWO), 1)
    used = lane < jnp.where(lane < WIDTH, count_ref[2 * g], WIDTH + count_ref[2 * g + 1])
    masked = [jnp.where(used, control_ref[t], 0.0) for t in range(slots)]
    for m0 in range(0, members, group):
        some = min(group, members - m0)
        n = some * levels
        rows = []
        for m in range(m0, m0 + some):
            w = ens_ref[m, 0].astype(F32) * masked[0]
            for t in range(1, slots):
                w = w + ens_ref[m, t].astype(F32) * masked[t]
            rows.append(w)
        w = jnp.concatenate(rows, axis=0)
        high = w.astype(BF16)
        low = (w - high.astype(F32)).astype(BF16)
        vh = vert[0, :n, :n]
        vl = vert[1, :n, :n]
        out = (dot(vh, low) + dot(vl, high) + dot(vh, high)).astype(BF16)
        at = pl.ds(m0 * levels, n)
        lifted[at, pl.ds(pl.multiple_of(g * TWO, TWO), TWO)] = out
        own_ref[at, :] = out

        @pl.when(odd)
        def _():
            pay3_ref[2 * g, at, :] = out[:, :WIDTH]
            pay3_ref[2 * g + 1, at, :] = out[:, WIDTH:]

        @pl.when(jnp.logical_not(odd))
        def _():
            pay1_ref[2 * g, at, :] = out[:, :WIDTH]
            pay1_ref[2 * g + 1, at, :] = out[:, WIDTH:]

    def store(ii, offset, value):
        row = pl.multiple_of(g * TWO + ii * WIDTH, WIDTH)
        col = pl.multiple_of((2 * g + offset) * WIDTH, WIDTH)
        band[pl.ds(row, WIDTH), pl.ds(col, WIDTH)] = value

    fill_band(pairs_ref, loc_ref, g, per, blocks, store)

    @pl.when(g == DEV // 2 - 1)
    def _():
        for q in range(DEV, DEV + SPAN, 2):
            first = max(0, q - SPAN) * WIDTH
            c = dot(lifted[:, first:], band[first:, q * WIDTH:(q + 2) * WIDTH])
            cb = c.astype(BF16)

            @pl.when(odd)
            def _():
                for e in range(2):
                    if q < 12:
                        mrg_ref[q - 8 + e] = c[:, e * WIDTH:(e + 1) * WIDTH]
                    else:
                        pay1_ref[(q - 8 if q < 16 else q - 16) + e] = cb[:, e * WIDTH:(e + 1) * WIDTH]

            @pl.when(jnp.logical_not(odd))
            def _():
                for e in range(2):
                    pay3_ref[q - 8 + e] = cb[:, e * WIDTH:(e + 1) * WIDTH]


def near_kernel(per, blocks, pairs_ref, loc_ref, own_ref, acc_ref, band_ref):
    step = pl.program_id(0)

    def store(ii, offset, value):
        col = pl.multiple_of((offset + 2) * WIDTH, WIDTH)
        band_ref[0, ii * WIDTH:(ii + 1) * WIDTH, pl.ds(col, WIDTH)] = value

    fill_band(pairs_ref, loc_ref, step, per, blocks, store)
    for g in range(DEV // 2):
        @pl.when(step == g)
        def _():
            c0 = g * TWO
            mine = own_ref[:, c0:c0 + TWO]
            to_first = dot_t(own_ref[:, c0:], band_ref[0, :, TWO:TWO + DEV * WIDTH - c0])
            cross = dot(mine[:, :WIDTH], band_ref[0, :WIDTH, TWO + WIDTH:2 * TWO])
            if g == 0:
                acc_ref[:, :WIDTH] = to_first[:, :WIDTH]
                acc_ref[:, WIDTH:TWO] = to_first[:, WIDTH:] + cross
            else:
                acc_ref[:, c0:c0 + WIDTH] += to_first[:, :WIDTH]
                acc_ref[:, c0 + WIDTH:c0 + TWO] += to_first[:, WIDTH:] + cross
            if g < DEV // 2 - 1:
                to_second = dot(mine, band_ref[0, :, 2 * TWO:TWO + DEV * WIDTH - c0])
                if g == 0:
                    acc_ref[:, TWO:] = to_second
                else:
                    acc_ref[:, c0 + TWO:] += to_second


def merge_kernel(pairs_ref, mrg_ref, head_ref, tail_ref, out_ref):
    odd = is_odd(pairs_ref)

    @pl.when(odd)
    def _():
        out_ref[...] = (mrg_ref[...] + tail_ref[...].astype(F32)).astype(BF16)

    @pl.when(jnp.logical_not(odd))
    def _():
        out_ref[...] = head_ref[...]


def far_kernel(pairs_ref, r1_ref, r3_ref, band_ref, acc_ref, out_ref, far):
    step = pl.program_id(0)
    odd = is_odd(pairs_ref)

    @pl.when(jnp.logical_and(step == 0, odd))
    def _():
        for b in range(DEV):
            far[:, b * WIDTH:(b + 1) * WIDTH] = r1_ref[b]

    @pl.when(jnp.logical_and(step == 0, jnp.logical_not(odd)))
    def _():
        for b in range(DEV):
            far[:, b * WIDTH:(b + 1) * WIDTH] = r3_ref[b]

    for g in range(DEV // 2):
        @pl.when(step == g)
        def _():
            last = min(DEV, 2 * g + SPAN + 2 - DEV)
            start = (DEV - 2 * g + 2) * WIDTH
            out_ref[...] = acc_ref[...] + dot_t(far[:, :last * WIDTH], band_ref[0, :, start:start + last * WIDTH])


def mix_kernel(members, slots, levels, members_all, pairs_ref, count_ref, ens_ref, acc_ref, band_ref, r1_ref, r3_ref,
               r1b_ref, r3b_ref, out_ref, spread):
    g = pl.program_id(0)
    odd = is_odd(pairs_ref)
    even = jnp.logical_not(odd)
    spread[...] = acc_ref[...]

    @pl.when(g >= 2)
    def _():
        def add2(x_ref):
            for e in range(2):
                spread[...] += dot_t(x_ref[e], band_ref[0, :, (e + 2) * WIDTH:(e + 3) * WIDTH])

        def add4(x_ref):
            for e in range(4):
                spread[...] += dot_t(x_ref[e], band_ref[0, :, e * WIDTH:(e + 1) * WIDTH])

        for flag, ref in ((odd, r1b_ref), (even, r3b_ref)):
            @pl.when(jnp.logical_and(flag, g == 2))
            def _():
                add2(ref)

            @pl.when(jnp.logical_and(flag, g == 3))
            def _():
                add4(ref)

    for e in range(2):
        cols = pl.ds(e * WIDTH, WIDTH)

        @pl.when(odd)
        def _():
            spread[:, cols] += r3_ref[e].astype(F32)

        @pl.when(jnp.logical_and(odd, g < 2))
        def _():
            spread[:, cols] += r3b_ref[2 * jnp.minimum(g, 1) + e].astype(F32)

        @pl.when(jnp.logical_and(even, g < 2))
        def _():
            spread[:, cols] += r1b_ref[2 * jnp.minimum(g, 1) + e].astype(F32)

        @pl.when(jnp.logical_and(even, g >= 2))
        def _():
            spread[:, cols] += r1_ref[e].astype(F32)

    lane = lax.broadcasted_iota(jnp.int32, (levels, WIDTH), 1)
    for e in range(2):
        cols = pl.ds(e * WIDTH, WIDTH)
        used = lane < count_ref[2 * g + e]
        totals = [jnp.zeros((levels, WIDTH), F32) for _ in range(slots)]
        for m in range(members):
            s = spread[m * levels:(m + 1) * levels, cols]
            for t in range(slots):
                totals[t] = totals[t] + ens_ref[m, t, :, cols].astype(F32) * s
        for t in range(slots):
            out_ref[e, t] = jnp.where(used, totals[t] / (members_all - 1), 0.0).astype(BF16)


def params(mib):
    return pltpu.CompilerParams(vmem_limit_bytes=mib << 20, dimension_semantics=("arbitrary",))


def per_device(ens, control, col_count, level_index, pair_blocks, loc_blocks):
    blocks_dev = col_count.shape[0]
    per = pair_blocks.shape[0] // blocks_dev
    peers = lax.axis_size("grid")
    blocks = peers * blocks_dev
    members, slots, levels, columns = ens.shape
    members_all = members * lax.axis_size("mem")
    rows = members * levels
    assert blocks_dev == DEV and columns == DEV * WIDTH and per == SPAN and peers % 2 == 0
    pairs = pair_blocks.T
    steps = DEV // 2
    one = lambda shape: pl.BlockSpec(shape, lambda g: (0,) * len(shape))
    ens_spec = pl.BlockSpec((members, slots, levels, TWO), lambda g: (0, 0, 0, g))
    loc_spec = pl.BlockSpec((2 * per, WIDTH, WIDTH), lambda g: (g, 0, 0))
    cols_spec = pl.BlockSpec((rows, TWO), lambda g: (0, g))
    full = lambda n, kind: jax.ShapeDtypeStruct((n, rows, WIDTH), kind)

    own, pay1, pay3, mrg = pl.pallas_call(
        functools.partial(lift_kernel, members, slots, levels, per, blocks),
        grid=(steps,),
        in_specs=[SMEM, SMEM, SMEM, ens_spec, pl.BlockSpec((slots, levels, TWO), lambda g: (0, 0, g)), loc_spec],
        out_specs=[cols_spec, one((8, rows, WIDTH)), one((12, rows, WIDTH)), one((4, rows, WIDTH))],
        out_shape=[jax.ShapeDtypeStruct((rows, columns), BF16), full(8, BF16), full(12, BF16), full(4, F32)],
        scratch_shapes=[
            pltpu.VMEM((rows, columns), BF16),
            pltpu.VMEM((columns, (DEV + SPAN) * WIDTH), BF16),
            pltpu.VMEM((2, WIDTH, WIDTH), BF16),
        ],
        compiler_params=params(32),
        name="lift",
    )(pairs, col_count, level_index, ens, control, loc_blocks)

    chips = [(i, (i + 1) % peers if i % 2 else (i - 1) % peers) for i in range(peers)]
    cores = [(i, i ^ 1) for i in range(peers)]
    r1 = lax.ppermute(pay1, "grid", chips)
    r3 = lax.ppermute(pay3, "grid", cores)

    acc, band = pl.pallas_call(
        functools.partial(near_kernel, per, blocks),
        grid=(steps,),
        in_specs=[SMEM, loc_spec, one((rows, columns))],
        out_specs=[one((rows, columns)), pl.BlockSpec((1, TWO, LANES), lambda g: (g, 0, 0))],
        out_shape=[jax.ShapeDtypeStruct((rows, columns), F32), jax.ShapeDtypeStruct((steps, TWO, LANES), BF16)],
        compiler_params=params(24),
        cost_estimate=pl.CostEstimate(flops=2 * 60 * rows * WIDTH * WIDTH, bytes_accessed=10 << 20, transcendentals=0),
        name="near",
    )(pairs, loc_blocks, own)

    pay1b = pl.pallas_call(
        merge_kernel,
        grid=(1,),
        in_specs=[SMEM, one((4, rows, WIDTH)), one((4, rows, WIDTH)),
                  pl.BlockSpec((4, rows, WIDTH), lambda g: (2, 0, 0))],
        out_specs=one((4, rows, WIDTH)),
        out_shape=full(4, BF16),
        compiler_params=params(12),
        name="merge",
    )(pairs, mrg, r3, r3)
    r1b = lax.ppermute(pay1b, "grid", chips)
    r3b = lax.ppermute(r1[:4], "grid", cores)

    acc = pl.pallas_call(
        far_kernel,
        grid=(steps,),
        in_specs=[SMEM, one((8, rows, WIDTH)), one((8, rows, WIDTH)),
                  pl.BlockSpec((1, TWO, LANES), lambda g: (g, 0, 0)), cols_spec],
        out_specs=cols_spec,
        out_shape=jax.ShapeDtypeStruct((rows, columns), F32),
        scratch_shapes=[pltpu.VMEM((rows, columns), BF16)],
        compiler_params=params(24),
        cost_estimate=pl.CostEstimate(flops=2 * 60 * rows * WIDTH * WIDTH, bytes_accessed=6 << 20, transcendentals=0),
        name="far",
    )(pairs, r1, r3, band, acc)

    two_blocks = pl.BlockSpec((2, rows, WIDTH), lambda g: (g, 0, 0))
    terms = pl.pallas_call(
        functools.partial(mix_kernel, members, slots, levels, members_all),
        grid=(steps,),
        in_specs=[SMEM, SMEM, ens_spec, cols_spec, pl.BlockSpec((1, TWO, 4 * WIDTH), lambda g: (g, 0, 3)),
                  two_blocks, two_blocks, one((4, rows, WIDTH)), one((4, rows, WIDTH))],
        out_specs=pl.BlockSpec((2, slots, levels, WIDTH), lambda g: (g, 0, 0, 0)),
        out_shape=jax.ShapeDtypeStruct((DEV, slots, levels, WIDTH), BF16),
        scratch_shapes=[pltpu.VMEM((rows, TWO), F32)],
        compiler_params=params(24),
        name="mix",
    )(pairs, col_count, ens, acc, band, r1, r3, r1b, r3b)
    parts = lax.all_to_all(terms, "mem", 0, 0, tiled=True)
    return jnp.sum(parts.astype(F32), axis=0)


def solution(mesh):
    return jax.shard_map(
        per_device,
        mesh=mesh,
        in_specs=(
            P("mem", None, None, "grid"),
            P(None, None, "grid"),
            P("grid"),
            P(),
            P("grid", None),
            P("grid", None, None),
        ),
        out_specs=P(None, None, ("grid", "mem")),
        check_vma=False,
    )
```

time: 262 us -> 72.9 us (0.28)
  the two profiles are of different devices: /device:TPU:6 before, /device:TPU:8 now
where the time goes in v1:
time: 72.9 us; the launch traced here: 72.5 us
  starting transfers between devices  24.4 us (33%)
  Pallas kernels  16.4 us (22%)
  blocking collectives  16 us (22%)
  waiting for transfers between devices  8.26 us (11%)
  local copies, waits for them, and re-layouts  6.69 us (9%)
    all_to_all x1, blocking collectives, per_device(): parts = lax.all_to_all(terms, 'mem', 0, 0, tiled=True)  16 us
    ppermute x1, starting transfers between devices, per_device(): r1 = lax.ppermute(pay1, 'grid', chips)  13.2 us
    ppermute x1, waiting for transfers between devices, per_device(): r1 = lax.ppermute(pay1, 'grid', chips)  8.25 us
    pallas_call x1, Pallas kernels, per_device(): pl.pallas_call(functools.partial(lift_kernel, members, slots, levels, per...  7.45 us
    ppermute x1, starting transfers between devices, per_device(): r1b = lax.ppermute(pay1b, 'grid', chips)  7.01 us
    unnamed x16, local copies, waits for them, and re-layouts  6.67 us
    pallas_call x1, Pallas kernels, per_device(): pl.pallas_call(functools.partial(near_kernel, per, blocks), grid=(steps,)...  3.24 us
    pallas_call x1, Pallas kernels, per_device(): pl.pallas_call(far_kernel, grid=(steps,), in_specs=[SMEM, one((8, rows, W...  2.59 us
  transfers between devices with their start and end apart: 4, of which 1 were waited for; matrix products, arithmetic and copies ran while one was open for 0% of the time, Pallas kernels for 9%

profile of v1, /device:TPU:8, one launch (start us, length us, event | category | flops | bytes accessed | tf_op | source)
XLA Modules:
  0.0 72.5 jit_solution(12168358910490626553)
XLA Ops:
  0.0 0.0 copy-start
  0.0 1.9 %copy-done = bf16[96,128,128]{2,1,0:T(8,128)(2,1)S(1)} copy-done((bf16[96,128,128]{2,1,0:T(8,128)(2,1)S(1)}, bf16[96,128,128]{2,1,0:T(8,128)(2,1)}, u32[]{:S(2)}) %copy-start) | copy-done | bytes 3145752
  1.9 0.0 copy-start.2
  1.9 1.7 %copy-done.2 = bf16[10,4,32,1024]{3,2,1,0:T(8,128)(2,1)S(1)} copy-done((bf16[10,4,32,1024]{3,2,1,0:T(8,128)(2,1)S(1)}, bf16[10,4,32,1024]{3,2,1,0:T(8,128)(2,1)}, u32[]{:S(2)}) %copy-start.2) | copy-done | bytes 2621464
  3.6 0.0 copy-start.4
  3.6 1.0 %copy-done.4 = f32[4,32,1024]{2,1,0:T(8,128)S(1)} copy-done((f32[4,32,1024]{2,1,0:T(8,128)S(1)}, f32[4,32,1024]{2,1,0:T(8,128)}, u32[]{:S(2)}) %copy-start.4) | copy-done | bytes 524312
  4.7 0.0 copy-start.5
  4.7 0.7 copy-done.5
  5.4 0.0 copy-start.6
  5.4 0.7 copy-done.6
  6.0 0.0 copy-start.7
  6.0 0.7 copy-done.7
  6.7 7.4 %lift.1 = (bf16[320,1024]{1,0:T(8,128)(2,1)S(1)}, bf16[8,320,128]{2,1,0:T(8,128)(2,1)S(1)}, bf16[12,320,128]{2,1,0:T(8,128)(2,1)S(1)}, f32[4,320,128]{2,1,0:T(8,128)S(1)}) custom-call(s32[2,96]{1,0:T(2,128)S(1)} %bitcast.1, s32[8]{0:T(128)S(1)} %copy-done.6, s32[32]{0:T(128)S(1)} %copy-done.7, bf16[10,4,32,1024]{3,2,1,0:T(8,128)(2,1)S(1)} %copy-done.2, ...), custom_call_target="tpu_custom_call" | custom-call | tf_op jit(solution)/shard_map/lift/pallas_call | solution.py:275
  14.1 0.0 copy-start.1
  14.1 2.2 %collective-permute-start.1 = (bf16[12,320,128]{2,1,0:T(8,128)(2,1)S(1)}, bf16[12,320,128]{2,1,0:T(8,128)(2,1)S(1)}, u32[]{:S(2)}, u32[]{:S(2)}) collective-permute-start(bf16[12,320,128]{2,1,0:T(8,128)(2,1)S(1)} %get-tuple-element.12), channel_id=1, source_target_pairs={{0,8},{8,0},{16,24},{24,16},{32,40},{40,32},{48,56},{56,48},{64,72... | collective-permute-start | bytes 2949128 | tf_op jit(solution)/shard_map/ppermute | solution.py:293
  16.3 13.2 %collective-permute-start = (bf16[8,320,128]{2,1,0:T(8,128)(2,1)S(1)}, bf16[8,320,128]{2,1,0:T(8,128)(2,1)S(1)}, u32[]{:S(2)}, u32[]{:S(2)}) collective-permute-start(bf16[8,320,128]{2,1,0:T(8,128)(2,1)S(1)} %get-tuple-element.11), channel_id=1, source_target_pairs={{0,504},{8,16},{16,8},{24,32},{32,24},{40,48},{48,40},{56,64},{64,... | collective-permute-start | bytes 1966088 | tf_op jit(solution)/shard_map/ppermute | solution.py:292
  29.6 8.3 %collective-permute-done.r1_ref = bf16[8,320,128]{2,1,0:T(8,128)(2,1)S(1)} collective-permute-done((bf16[8,320,128]{2,1,0:T(8,128)(2,1)S(1)}, bf16[8,320,128]{2,1,0:T(8,128)(2,1)S(1)}, u32[]{:S(2)}, u32[]{:S(2)}) %collective-permute-start) | collective-permute-done | bytes 655392 | tf_op jit(solution)/shard_map/ppermute | solution.py:292
  37.9 1.9 %collective-permute-start.3 = (bf16[4,320,128]{2,1,0:T(8,128)(2,1)S(1)}, bf16[4,320,128]{2,1,0:T(8,128)(2,1)S(1)}, u32[]{:S(2)}, u32[]{:S(2)}) collective-permute-start(bf16[4,320,128]{2,1,0:T(8,128)(2,1)S(1)} %slice.4), channel_id=1, source_target_pairs={{0,8},{8,0},{16,24},{24,16},{32,40},{40,32},{48,56},{56,48},{64,72... | collective-permute-start | bytes 983048 | tf_op jit(solution)/shard_map/ppermute | solution.py:317
  39.8 0.0 collective-permute-done.1.r3_ref.head_ref.tail_ref
  39.8 0.6 merge.1
  40.4 7.0 %collective-permute-start.2 = (bf16[4,320,128]{2,1,0:T(8,128)(2,1)S(1)}, bf16[4,320,128]{2,1,0:T(8,128)(2,1)S(1)}, u32[]{:S(2)}, u32[]{:S(2)}) collective-permute-start(bf16[4,320,128]{2,1,0:T(8,128)(2,1)S(1)} %merge.1), channel_id=1, source_target_pairs={{0,504},{8,16},{16,8},{24,32},{32,24},{40,48},{48,40},{56,64},{64,... | collective-permute-start | bytes 983048 | tf_op jit(solution)/shard_map/ppermute | solution.py:316
  47.4 0.0 copy-done.1
  47.4 3.2 %near.1 = (f32[320,1024]{1,0:T(8,128)S(1)}, bf16[4,256,2048]{2,1,0:T(8,128)(2,1)S(1)}) custom-call(s32[2,96]{1,0:T(2,128)S(1)} %bitcast.3, bf16[96,128,128]{2,1,0:T(8,128)(2,1)S(1)} %copy-done.1, bf16[320,1024]{1,0:T(8,128)(2,1)S(1)} %get-tuple-element.13.own_ref), custom_call_target="tpu_custom_call" | custom-call | flops 629145600 | bytes 10485760 | tf_op jit(solution)/shard_map/near/pallas_call | solution.py:295
  50.7 0.0 copy-start.3
  50.7 2.6 %far.1.acc_ref = f32[320,1024]{1,0:T(8,128)S(1)} custom-call(s32[2,96]{1,0:T(2,128)S(1)} %bitcast.4, bf16[8,320,128]{2,1,0:T(8,128)(2,1)S(1)} %collective-permute-done.r1_ref, bf16[12,320,128]{2,1,0:T(8,128)(2,1)S(1)} %collective-permute-done.1.r3_ref.head_ref.tail_ref, bf16[4,256,2048]{2,1,0:T(8,128)(2,1)S(1)} %get-tuple-element.14.band_ref, ...), custom_call_target="tpu_custom_call" | custom-call | flops 629145600 | bytes 6291456 | tf_op jit(solution)/shard_map/far/pallas_call | solution.py:319
  53.3 0.0 collective-permute-done.3.r3b_ref
  53.3 0.0 collective-permute-done.2.r1b_ref
  53.3 0.0 copy-done.3
  53.3 2.6 %mix.1 = bf16[8,4,32,128]{3,2,1,0:T(8,128)(2,1)S(1)} custom-call(s32[2,96]{1,0:T(2,128)S(1)} %bitcast.5, s32[8]{0:T(128)S(1)} %copy-done.6, bf16[10,4,32,1024]{3,2,1,0:T(8,128)(2,1)S(1)} %copy-done.3, f32[320,1024]{1,0:T(8,128)S(1)} %far.1.acc_ref, bf16[4,256,2048]{2,1,0:T(8,128)(2,1)S(1)} %get-tuple-element.14.band_ref, ...), custom_call_target="tpu_custom_call" | custom-call | tf_op jit(solution)/shard_map/mix/pallas_call | solution.py:333
  55.9 16.0 %all_to_all.5 = bf16[8,4,32,128]{3,2,1,0:T(8,128)(2,1)S(1)} all-to-all(bf16[8,4,32,128]{3,2,1,0:T(8,128)(2,1)S(1)} %mix.1), channel_id=1, replica_groups=mesh['grid'=64,'mem'=8] {'mem'}, dimensions={0} | all-to-all | bytes 524288 | tf_op jit(solution)/shard_map/all_to_all | solution.py:344
  71.8 0.7 convert_reduce_fusion
  (1 shorter events, 0.0 us)
Async XLA Ops:
  0.0 1.9 %copy-start = (bf16[96,128,128]{2,1,0:T(8,128)(2,1)S(1)}, bf16[96,128,128]{2,1,0:T(8,128)(2,1)}, u32[]{:S(2)}) copy-start(bf16[96,128,128]{2,1,0:T(8,128)(2,1)} %loc_ref.3) | copy-start | bytes 9437188
  1.9 1.7 %copy-start.2 = (bf16[10,4,32,1024]{3,2,1,0:T(8,128)(2,1)S(1)}, bf16[10,4,32,1024]{3,2,1,0:T(8,128)(2,1)}, u32[]{:S(2)}) copy-start(bf16[10,4,32,1024]{3,2,1,0:T(8,128)(2,1)} %ens_ref.3) | copy-start | bytes 7864324
  3.6 1.0 %copy-start.4 = (f32[4,32,1024]{2,1,0:T(8,128)S(1)}, f32[4,32,1024]{2,1,0:T(8,128)}, u32[]{:S(2)}) copy-start(f32[4,32,1024]{2,1,0:T(8,128)} %control_ref.1) | copy-start | bytes 1572868
  4.7 0.7 copy-start.5
  5.4 0.7 copy-start.6
  6.0 0.7 copy-start.7
  14.1 33.3 %copy-start.1 = (bf16[96,128,128]{2,1,0:T(8,128)(2,1)S(1)}, bf16[96,128,128]{2,1,0:T(8,128)(2,1)}, u32[]{:S(2)}) copy-start(bf16[96,128,128]{2,1,0:T(8,128)(2,1)} %loc_ref.3) | copy-start | bytes 9437188
  14.1 25.7 %collective-permute-start.1 = (bf16[12,320,128]{2,1,0:T(8,128)(2,1)S(1)}, bf16[12,320,128]{2,1,0:T(8,128)(2,1)S(1)}, u32[]{:S(2)}, u32[]{:S(2)}) collective-permute-start(bf16[12,320,128]{2,1,0:T(8,128)(2,1)S(1)} %get-tuple-element.12), channel_id=1, source_target_pairs={{0,8},{8,0},{16,24},{24,16},{32,40},{40,32},{48,56},{56,48},{64,72... | collective-permute-start | bytes 2949128 | tf_op jit(solution)/shard_map/ppermute | solution.py:293
  16.3 21.5 %collective-permute-start = (bf16[8,320,128]{2,1,0:T(8,128)(2,1)S(1)}, bf16[8,320,128]{2,1,0:T(8,128)(2,1)S(1)}, u32[]{:S(2)}, u32[]{:S(2)}) collective-permute-start(bf16[8,320,128]{2,1,0:T(8,128)(2,1)S(1)} %get-tuple-element.11), channel_id=1, source_target_pairs={{0,504},{8,16},{16,8},{24,32},{32,24},{40,48},{48,40},{56,64},{64,... | collective-permute-start | bytes 1966088 | tf_op jit(solution)/shard_map/ppermute | solution.py:292
  37.9 15.4 %collective-permute-start.3 = (bf16[4,320,128]{2,1,0:T(8,128)(2,1)S(1)}, bf16[4,320,128]{2,1,0:T(8,128)(2,1)S(1)}, u32[]{:S(2)}, u32[]{:S(2)}) collective-permute-start(bf16[4,320,128]{2,1,0:T(8,128)(2,1)S(1)} %slice.4), channel_id=1, source_target_pairs={{0,8},{8,0},{16,24},{24,16},{32,40},{40,32},{48,56},{56,48},{64,72... | collective-permute-start | bytes 983048 | tf_op jit(solution)/shard_map/ppermute | solution.py:317
  40.4 12.9 %collective-permute-start.2 = (bf16[4,320,128]{2,1,0:T(8,128)(2,1)S(1)}, bf16[4,320,128]{2,1,0:T(8,128)(2,1)S(1)}, u32[]{:S(2)}, u32[]{:S(2)}) collective-permute-start(bf16[4,320,128]{2,1,0:T(8,128)(2,1)S(1)} %merge.1), channel_id=1, source_target_pairs={{0,504},{8,16},{16,8},{24,32},{32,24},{40,48},{48,40},{56,64},{64,... | collective-permute-start | bytes 983048 | tf_op jit(solution)/shard_map/ppermute | solution.py:316
  50.7 2.6 %copy-start.3 = (bf16[10,4,32,1024]{3,2,1,0:T(8,128)(2,1)S(1)}, bf16[10,4,32,1024]{3,2,1,0:T(8,128)(2,1)}, u32[]{:S(2)}) copy-start(bf16[10,4,32,1024]{3,2,1,0:T(8,128)(2,1)} %ens_ref.3) | copy-start | bytes 7864324

commit v2 on v0

v2 whole, which is shorter than its diff:
```python
import functools

import jax
import jax.numpy as jnp
from jax import lax
from jax.experimental import pallas as pl
from jax.experimental.pallas import tpu as pltpu
from jax.sharding import PartitionSpec as P

SPAN = 12
WIDTH = 128
DEV = 8
QUAD = 4 * WIDTH

vertical_scale = 8.0

F32 = jnp.float32
BF16 = jnp.bfloat16
VMEM = pl.BlockSpec(memory_space=pltpu.VMEM)
HBM = pl.BlockSpec(memory_space=pltpu.HBM)


def dot(a, b):
    return lax.dot_general(a, b, (((1,), (0,)), ((), ())), preferred_element_type=F32)


def dot_t(a, b):
    return lax.dot_general(a, b, (((1,), (1,)), ((), ())), preferred_element_type=F32)


def block(b):
    return slice(b * WIDTH, (b + 1) * WIDTH)


def by_core(first, second):
    odd = lax.rem(lax.axis_index("grid"), 2) == 1
    pl.when(jnp.logical_not(odd))(first)
    pl.when(odd)(second)


def lift_kernel(per, blocks, pairs_hbm, count_hbm, level_hbm, ens_hbm, control_hbm, loc_hbm,
                own_ref, band_ref, ens_ref, live_ref, pay1_ref,
                pairs_ref, count_ref, level_ref, control_ref, loc_ref, vert, sems):
    members, slots, levels, columns = ens_ref.shape
    group = WIDTH // levels
    cuts = [(m, min(group, members - m)) for m in range(0, members, group)]
    scalars = [
        pltpu.make_async_copy(level_hbm, level_ref, sems.at[0]),
        pltpu.make_async_copy(count_hbm, count_ref, sems.at[1]),
        pltpu.make_async_copy(pairs_hbm, pairs_ref, sems.at[2]),
    ]
    control_copy = pltpu.make_async_copy(control_hbm, control_ref, sems.at[3])
    ens_copies = [
        pltpu.make_async_copy(ens_hbm.at[pl.ds(m, n)], ens_ref.at[pl.ds(m, n)], sems.at[4 + i])
        for i, (m, n) in enumerate(cuts)
    ]
    some = 2 * per
    loc_copies = [
        pltpu.make_async_copy(loc_hbm.at[pl.ds(i * some, some)], loc_ref.at[pl.ds(i * some, some)], sems.at[8 + i])
        for i in range(DEV // 2)
    ]
    for copy in scalars + [control_copy] + ens_copies + loc_copies:
        copy.start()

    for i in range(DEV):
        low = i // 4 * 4
        for j in range(low, low + 16):
            if j < i or j > i + SPAN:
                band_ref[block(i), block(j)] = jnp.zeros((WIDTH, WIDTH), BF16)

    for copy in scalars:
        copy.wait()
    lane = lax.broadcasted_iota(jnp.int32, (levels, WIDTH), 1)
    row = lax.broadcasted_iota(jnp.int32, (levels, WIDTH), 0)
    by_lane = jnp.zeros((levels, WIDTH), F32)
    by_row = jnp.zeros((levels, WIDTH), F32)
    for l in range(levels):
        value = level_ref[l].astype(F32)
        by_lane = jnp.where(lane % levels == l, value, by_lane)
        by_row = jnp.where(row == l, value, by_row)
    v = jnp.exp(-jnp.abs(by_row - by_lane) / vertical_scale)
    for q in range(group):
        part = jnp.where(lane // levels == q, v, 0.0)
        high = part.astype(BF16)
        vert[0, q * levels:(q + 1) * levels, :] = high
        vert[1, q * levels:(q + 1) * levels, :] = (part - high.astype(F32)).astype(BF16)

    lane = lax.broadcasted_iota(jnp.int32, (DEV, WIDTH), 1)
    row = lax.broadcasted_iota(jnp.int32, (DEV, WIDTH), 0)
    limit = jnp.zeros((DEV, WIDTH), jnp.int32)
    for b in range(DEV):
        limit = jnp.where(row == b, count_ref[b], limit)
    live_ref[...] = (lane < limit).astype(F32)

    control_copy.wait()
    for b in range(DEV):
        control_ref[:, :, block(b)] = control_ref[:, :, block(b)] * live_ref[b:b + 1, :][None]

    for (m0, count), copy in zip(cuts, ens_copies):
        copy.wait()
        n = count * levels
        vh = vert[0, :n, :n]
        vl = vert[1, :n, :n]
        for c in range(0, columns, 2 * WIDTH):
            cols = slice(c, c + 2 * WIDTH)
            rows = []
            for m in range(m0, m0 + count):
                w = ens_ref[m, 0, :, cols].astype(F32) * control_ref[0, :, cols]
                for t in range(1, slots):
                    w = w + ens_ref[m, t, :, cols].astype(F32) * control_ref[t, :, cols]
                rows.append(w)
            w = jnp.concatenate(rows, axis=0)
            high = w.astype(BF16)
            low = (w - high.astype(F32)).astype(BF16)
            own_ref[m0 * levels:m0 * levels + n, cols] = (dot(vh, low) + dot(vl, high) + dot(vh, high)).astype(BF16)

    for i in range(DEV):
        if i % 2 == 0:
            loc_copies[i // 2].wait()
        left = SPAN * (SPAN + 1) // 2
        for p in range(i * per, (i + 1) * per):
            k = pairs_ref[1, p] - pairs_ref[0, p]
            k = jnp.where(k < 0, k + blocks, k)
            left = left - k
            band_ref[block(i), pl.ds(pl.multiple_of((i + k) * WIDTH, WIDTH), WIDTH)] = loc_ref[p]
        band_ref[block(i), pl.ds(pl.multiple_of((i + left) * WIDTH, WIDTH), WIDTH)] = jnp.zeros((WIDTH, WIDTH), BF16)

    def first():
        for b in range(DEV):
            pay1_ref[b] = own_ref[:, block(b)]

    def second():
        near = dot(own_ref[...], band_ref[:, 3 * QUAD:4 * QUAD]).astype(BF16)
        far = dot(own_ref[:, QUAD:], band_ref[QUAD:, 4 * QUAD:]).astype(BF16)
        for e in range(4):
            pay1_ref[e] = far[:, block(e)]
            pay1_ref[4 + e] = near[:, block(e)]

    by_core(first, second)


def reach_kernel(own_ref, band_ref, pay3_ref, mrg_ref):
    def first():
        for q in range(2, 5):
            start = QUAD if q == 4 else 0
            c = dot(own_ref[:, start:], band_ref[start:, q * QUAD:(q + 1) * QUAD]).astype(BF16)
            for e in range(4):
                pay3_ref[4 * (q - 2) + e] = c[:, block(e)]

    def second():
        c = dot(own_ref[...], band_ref[:, 2 * QUAD:3 * QUAD])
        for e in range(4):
            mrg_ref[e] = c[:, block(e)]
        for b in range(DEV):
            pay3_ref[b] = own_ref[:, block(b)]

    by_core(first, second)


def merge_kernel(mrg_ref, r3_ref, out_ref):
    def first():
        out_ref[...] = r3_ref[:4]

    def second():
        out_ref[...] = (mrg_ref[...] + r3_ref[8:].astype(F32)).astype(BF16)

    by_core(first, second)


def near_kernel(own_ref, band_ref, acc_ref, upper):
    for h in range(2):
        for i in range(4):
            for j in range(4):
                if j > i:
                    upper[h, block(i), block(j)] = band_ref[block(4 * h + i), block(4 * h + j)]
                else:
                    upper[h, block(i), block(j)] = jnp.zeros((WIDTH, WIDTH), BF16)
    acc_ref[:, :QUAD] = dot_t(own_ref[...], band_ref[:QUAD, :2 * QUAD])
    acc_ref[:, QUAD:] = dot_t(own_ref[:, QUAD:], band_ref[QUAD:, QUAD:2 * QUAD])
    acc_ref[:, :QUAD] += dot(own_ref[:, :QUAD], upper[0])
    acc_ref[:, QUAD:] += dot(own_ref[:, :QUAD], band_ref[:QUAD, QUAD:2 * QUAD])
    acc_ref[:, QUAD:] += dot(own_ref[:, QUAD:], upper[1])


def far_kernel(band_ref, acc_ref, r1_ref, r3_ref, out_ref, far):
    def first():
        for b in range(DEV):
            far[:, block(b)] = r3_ref[b]

    def second():
        for b in range(DEV):
            far[:, block(b)] = r1_ref[b]

    by_core(first, second)
    out_ref[...] = acc_ref[...] + dot_t(far[...], band_ref[:, 2 * QUAD:4 * QUAD])


def mix_kernel(members_all, ens_ref, band_ref, acc_ref, live_ref, r1_ref, r3_ref, r1b_ref, r3b_ref, out_ref,
               far, spread):
    members, slots, levels, columns = ens_ref.shape

    def first():
        for e in range(4):
            far[:, block(e)] = r3b_ref[e]
        for b in range(DEV):
            came = r1b_ref[b] if b < 4 else r1_ref[b]
            spread[:, block(b)] = acc_ref[:, block(b)] + came.astype(F32)

    def second():
        for e in range(4):
            far[:, block(e)] = r1b_ref[e]
        for b in range(DEV):
            came = r3_ref[b].astype(F32)
            if b < 4:
                came = came + r3b_ref[b].astype(F32)
            spread[:, block(b)] = acc_ref[:, block(b)] + came

    by_core(first, second)
    spread[:, QUAD:] += dot_t(far[...], band_ref[QUAD:, 4 * QUAD:])
    for b in range(DEV):
        totals = [jnp.zeros((levels, WIDTH), F32) for _ in range(slots)]
        for m in range(members):
            s = spread[m * levels:(m + 1) * levels, block(b)]
            for t in range(slots):
                totals[t] = totals[t] + ens_ref[m, t, :, block(b)].astype(F32) * s
        for t in range(slots):
            out_ref[b, t] = (totals[t] * live_ref[b:b + 1, :] / (members_all - 1)).astype(BF16)


def params(mib):
    return pltpu.CompilerParams(vmem_limit_bytes=mib << 20)


def per_device(ens, control, col_count, level_index, pair_blocks, loc_blocks):
    blocks_dev = col_count.shape[0]
    listed = pair_blocks.shape[0]
    per = listed // blocks_dev
    peers = lax.axis_size("grid")
    members, slots, levels, columns = ens.shape
    members_all = members * lax.axis_size("mem")
    rows = members * levels
    assert blocks_dev == DEV and columns == DEV * WIDTH and per == SPAN and peers % 2 == 0
    shape = jax.ShapeDtypeStruct
    pieces = lambda n, kind: shape((n, rows, WIDTH), kind)
    tie = lax.optimization_barrier

    args = (pair_blocks.T, col_count, level_index, ens, control, loc_blocks)
    own, band, ens_here, live, pay1 = pl.pallas_call(
        functools.partial(lift_kernel, per, peers * blocks_dev),
        in_specs=[HBM] * 6,
        out_specs=[VMEM] * 5,
        out_shape=[
            shape((rows, columns), BF16),
            shape((columns, (DEV + SPAN) * WIDTH), BF16),
            shape(ens.shape, BF16),
            shape((DEV, WIDTH), F32),
            pieces(8, BF16),
        ],
        scratch_shapes=[
            pltpu.SMEM((2, listed), jnp.int32),
            pltpu.SMEM(col_count.shape, jnp.int32),
            pltpu.SMEM(level_index.shape, jnp.int32),
            pltpu.VMEM(control.shape, F32),
            pltpu.VMEM(loc_blocks.shape, BF16),
            pltpu.VMEM((2, WIDTH, WIDTH), BF16),
            pltpu.SemaphoreType.DMA((12,)),
        ],
        compiler_params=params(28),
        name="lift",
    )(*[pltpu.with_memory_space_constraint(x, pltpu.HBM) for x in args])

    chips = [(i, (i + 1) % peers if i % 2 else (i - 1) % peers) for i in range(peers)]
    cores = [(i, i ^ 1) for i in range(peers)]
    r1 = lax.ppermute(pay1, "grid", chips)

    pay3, mrg = pl.pallas_call(
        reach_kernel,
        in_specs=[VMEM] * 2,
        out_specs=[VMEM] * 2,
        out_shape=[pieces(12, BF16), pieces(4, F32)],
        compiler_params=params(16),
        name="reach",
    )(own, band)
    r3 = lax.ppermute(pay3, "grid", cores)

    pay1b = pl.pallas_call(
        merge_kernel,
        in_specs=[VMEM] * 2,
        out_specs=VMEM,
        out_shape=pieces(4, BF16),
        compiler_params=params(12),
        name="merge",
    )(mrg, r3)
    r1b = lax.ppermute(pay1b, "grid", chips)

    own, pay1b = tie((own, pay1b))
    acc = pl.pallas_call(
        near_kernel,
        in_specs=[VMEM] * 2,
        out_specs=VMEM,
        out_shape=shape((rows, columns), F32),
        scratch_shapes=[pltpu.VMEM((2, QUAD, QUAD), BF16)],
        compiler_params=params(16),
        cost_estimate=pl.CostEstimate(flops=2 * 96 * rows * WIDTH * WIDTH, bytes_accessed=6 << 20, transcendentals=0),
        name="near",
    )(own, band)

    r1, acc = tie((r1, acc))
    r3b = lax.ppermute(r1[:4], "grid", cores)

    acc = pl.pallas_call(
        far_kernel,
        in_specs=[VMEM] * 4,
        out_specs=VMEM,
        out_shape=shape((rows, columns), F32),
        scratch_shapes=[pltpu.VMEM((rows, columns), BF16)],
        compiler_params=params(16),
        cost_estimate=pl.CostEstimate(flops=2 * 64 * rows * WIDTH * WIDTH, bytes_accessed=6 << 20, transcendentals=0),
        name="far",
    )(band, acc, r1, r3)

    terms = pl.pallas_call(
        functools.partial(mix_kernel, members_all),
        in_specs=[VMEM] * 8,
        out_specs=VMEM,
        out_shape=shape((DEV, slots, levels, WIDTH), BF16),
        scratch_shapes=[pltpu.VMEM((rows, QUAD), BF16), pltpu.VMEM((rows, columns), F32)],
        compiler_params=params(16),
        name="mix",
    )(ens_here, band, acc, live, r1, r3, r1b, r3b)
    parts = lax.all_to_all(terms, "mem", 0, 0, tiled=True)
    return jnp.sum(parts.astype(F32), axis=0)


def solution(mesh):
    return jax.shard_map(
        per_device,
        mesh=mesh,
        in_specs=(
            P("mem", None, None, "grid"),
            P(None, None, "grid"),
            P("grid"),
            P(),
            P("grid", None),
            P("grid", None, None),
        ),
        out_specs=P(None, None, ("grid", "mem")),
        check_vma=False,
    )
```

time: 262 us -> 52.8 us (0.20)
  the two profiles are of different devices: /device:TPU:6 before, /device:TPU:1 now
where the time goes in v2:
time: 52.8 us; the launch traced here: 52.6 us
  starting transfers between devices  19.9 us (38%)
  blocking collectives  17.9 us (34%)
  Pallas kernels  8.37 us (16%)
  waiting for transfers between devices  5.68 us (11%)
  other arithmetic  0.67 us (1%)
    all_to_all x1, blocking collectives, per_device(): parts = lax.all_to_all(terms, 'mem', 0, 0, tiled=True)  17.9 us
    ppermute x1, starting transfers between devices, per_device(): r3 = lax.ppermute(pay3, 'grid', cores)  8.73 us
    ppermute x1, starting transfers between devices, per_device(): r3b = lax.ppermute(r1[:4], 'grid', cores)  5.86 us
    ppermute x1, waiting for transfers between devices, per_device(): r1 = lax.ppermute(pay1, 'grid', chips)  5.29 us
    pallas_call x1, Pallas kernels, per_device(): pl.pallas_call(functools.partial(lift_kernel, per, peers * blocks_dev), i...  4.16 us
    ppermute x1, starting transfers between devices, per_device(): r1b = lax.ppermute(pay1b, 'grid', chips)  3.37 us
    ppermute x1, starting transfers between devices, per_device(): r1 = lax.ppermute(pay1, 'grid', chips)  1.92 us
    pallas_call x1, Pallas kernels, per_device(): pl.pallas_call(near_kernel, in_specs=[VMEM] * 2, out_specs=VMEM, out_shap...  1.26 us
  transfers between devices with their start and end apart: 4, of which 3 were waited for; matrix products, arithmetic and copies ran while one was open for 0% of the time, Pallas kernels for 5%

profile of v2, /device:TPU:1, one launch (start us, length us, event | category | flops | bytes accessed | tf_op | source)
XLA Modules:
  0.0 52.6 jit_solution(2257283686203738209)
XLA Ops:
  0.0 4.2 %lift.1 = (bf16[320,1024]{1,0:T(8,128)(2,1)S(1)}, bf16[1024,2560]{1,0:T(8,128)(2,1)S(1)}, bf16[10,4,32,1024]{3,2,1,0:T(8,128)(2,1)S(1)}, f32[8,128]{1,0:T(8,128)S(1)}, bf16[8,320,128]{2,1,0:T(8,128)(2,1)S(1)}) custom-call(s32[2,96]{1,0:T(2,128)} %bitcast.1, s32[8]{0:T(128)} %count_hbm.1, s32[32]{0:T(128)} %level_hbm.1, bf16[10,4,32,1024]{3,2,1,0:T(8,128)(2,1)} %ens_hbm.1, ...), custom_call_target="tpu_custom_call" | custom-call | tf_op jit(solution)/shard_map/lift/pallas_call | solution.py:248
  4.2 0.6 %reach.1 = (bf16[12,320,128]{2,1,0:T(8,128)(2,1)S(1)}, f32[4,320,128]{2,1,0:T(8,128)S(1)}) custom-call(bf16[320,1024]{1,0:T(8,128)(2,1)S(1)} %get-tuple-element.21.own_ref, bf16[1024,2560]{1,0:T(8,128)(2,1)S(1)} %get-tuple-element.16.band_ref), custom_call_target="tpu_custom_call" | custom-call | tf_op jit(solution)/shard_map/reach/pallas_call | solution.py:276
  4.7 8.7 %collective-permute-start.1 = (bf16[12,320,128]{2,1,0:T(8,128)(2,1)S(1)}, bf16[12,320,128]{2,1,0:T(8,128)(2,1)S(1)}, u32[]{:S(2)}, u32[]{:S(2)}) collective-permute-start(bf16[12,320,128]{2,1,0:T(8,128)(2,1)S(1)} %get-tuple-element.20), channel_id=1, source_target_pairs={{0,8},{8,0},{16,24},{24,16},{32,40},{40,32},{48,56},{56,48},{64,72... | collective-permute-start | bytes 2949128 | tf_op jit(solution)/shard_map/ppermute | solution.py:284
  13.5 1.9 %collective-permute-start = (bf16[8,320,128]{2,1,0:T(8,128)(2,1)S(1)}, bf16[8,320,128]{2,1,0:T(8,128)(2,1)S(1)}, u32[]{:S(2)}, u32[]{:S(2)}) collective-permute-start(bf16[8,320,128]{2,1,0:T(8,128)(2,1)S(1)} %get-tuple-element.17), channel_id=1, source_target_pairs={{0,504},{8,16},{16,8},{24,32},{32,24},{40,48},{48,40},{56,64},{64,... | collective-permute-start | bytes 1966088 | tf_op jit(solution)/shard_map/ppermute | solution.py:274
  15.4 0.2 collective-permute-done.1.r3_ref
  15.6 0.1 merge.1
  15.7 3.4 %collective-permute-start.2 = (bf16[4,320,128]{2,1,0:T(8,128)(2,1)S(1)}, bf16[4,320,128]{2,1,0:T(8,128)(2,1)S(1)}, u32[]{:S(2)}, u32[]{:S(2)}) collective-permute-start(bf16[4,320,128]{2,1,0:T(8,128)(2,1)S(1)} %merge.1), channel_id=1, source_target_pairs={{0,504},{8,16},{16,8},{24,32},{32,24},{40,48},{48,40},{56,64},{64,... | collective-permute-start | bytes 983048 | tf_op jit(solution)/shard_map/ppermute | solution.py:294
  19.1 1.3 %near.1.acc_ref = f32[320,1024]{1,0:T(8,128)S(1)} custom-call(bf16[320,1024]{1,0:T(8,128)(2,1)S(1)} %get-tuple-element.21.own_ref, bf16[1024,2560]{1,0:T(8,128)(2,1)S(1)} %get-tuple-element.16.band_ref), custom_call_target="tpu_custom_call" | custom-call | flops 1006632960 | bytes 6291456 | tf_op jit(solution)/shard_map/near/pallas_call | solution.py:297
  20.4 5.3 %collective-permute-done.r1_ref = bf16[8,320,128]{2,1,0:T(8,128)(2,1)S(1)} collective-permute-done((bf16[8,320,128]{2,1,0:T(8,128)(2,1)S(1)}, bf16[8,320,128]{2,1,0:T(8,128)(2,1)S(1)}, u32[]{:S(2)}, u32[]{:S(2)}) %collective-permute-start) | collective-permute-done | bytes 655392 | tf_op jit(solution)/shard_map/ppermute | solution.py:274
  25.7 5.9 %collective-permute-start.3 = (bf16[4,320,128]{2,1,0:T(8,128)(2,1)S(1)}, bf16[4,320,128]{2,1,0:T(8,128)(2,1)S(1)}, u32[]{:S(2)}, u32[]{:S(2)}) collective-permute-start(bf16[4,320,128]{2,1,0:T(8,128)(2,1)S(1)} %slice.3), channel_id=1, source_target_pairs={{0,8},{8,0},{16,24},{24,16},{32,40},{40,32},{48,56},{56,48},{64,72... | collective-permute-start | bytes 983048 | tf_op jit(solution)/shard_map/ppermute | solution.py:309
  31.6 1.1 %far.1.acc_ref = f32[320,1024]{1,0:T(8,128)S(1)} custom-call(bf16[1024,2560]{1,0:T(8,128)(2,1)S(1)} %get-tuple-element.16.band_ref, f32[320,1024]{1,0:T(8,128)S(1)} %near.1.acc_ref, bf16[8,320,128]{2,1,0:T(8,128)(2,1)S(1)} %collective-permute-done.r1_ref, bf16[12,320,128]{2,1,0:T(8,128)(2,1)S(1)} %collective-permute-done.1.r3_ref), custom_call_target="tpu_custom_call" | custom-call | flops 671088640 | bytes 6291456 | tf_op jit(solution)/shard_map/far/pallas_call | solution.py:311
  32.6 0.0 collective-permute-done.2.r1b_ref
  32.6 0.1 collective-permute-done.3.r3b_ref
  32.8 1.2 %mix.1 = bf16[8,4,32,128]{3,2,1,0:T(8,128)(2,1)S(1)} custom-call(bf16[10,4,32,1024]{3,2,1,0:T(8,128)(2,1)S(1)} %get-tuple-element.15.ens_ref, bf16[1024,2560]{1,0:T(8,128)(2,1)S(1)} %get-tuple-element.16.band_ref, f32[320,1024]{1,0:T(8,128)S(1)} %far.1.acc_ref, f32[8,128]{1,0:T(8,128)S(1)} %get-tuple-element.24.live_ref, ...), custom_call_target="tpu_custom_call" | custom-call | tf_op jit(solution)/shard_map/mix/pallas_call | solution.py:322
  34.0 17.9 %all_to_all.5 = bf16[8,4,32,128]{3,2,1,0:T(8,128)(2,1)S(1)} all-to-all(bf16[8,4,32,128]{3,2,1,0:T(8,128)(2,1)S(1)} %mix.1), channel_id=1, replica_groups=mesh['grid'=64,'mem'=8] {'mem'}, dimensions={0} | all-to-all | bytes 524288 | tf_op jit(solution)/shard_map/all_to_all | solution.py:331
  51.9 0.7 %convert_reduce_fusion = f32[4,32,128]{2,1,0:T(8,128)} fusion(bf16[8,4,32,128]{3,2,1,0:T(8,128)(2,1)S(1)} %all_to_all.5), kind=kLoop, calls=%fused_computation | loop fusion | flops 245760 | bytes 327680 | tf_op jit(solution)/shard_map/reduce_sum | solution.py:332
  (1 shorter events, 0.0 us)
Async XLA Ops:
  4.7 10.9 %collective-permute-start.1 = (bf16[12,320,128]{2,1,0:T(8,128)(2,1)S(1)}, bf16[12,320,128]{2,1,0:T(8,128)(2,1)S(1)}, u32[]{:S(2)}, u32[]{:S(2)}) collective-permute-start(bf16[12,320,128]{2,1,0:T(8,128)(2,1)S(1)} %get-tuple-element.20), channel_id=1, source_target_pairs={{0,8},{8,0},{16,24},{24,16},{32,40},{40,32},{48,56},{56,48},{64,72... | collective-permute-start | bytes 2949128 | tf_op jit(solution)/shard_map/ppermute | solution.py:284
  13.5 12.2 %collective-permute-start = (bf16[8,320,128]{2,1,0:T(8,128)(2,1)S(1)}, bf16[8,320,128]{2,1,0:T(8,128)(2,1)S(1)}, u32[]{:S(2)}, u32[]{:S(2)}) collective-permute-start(bf16[8,320,128]{2,1,0:T(8,128)(2,1)S(1)} %get-tuple-element.17), channel_id=1, source_target_pairs={{0,504},{8,16},{16,8},{24,32},{32,24},{40,48},{48,40},{56,64},{64,... | collective-permute-start | bytes 1966088 | tf_op jit(solution)/shard_map/ppermute | solution.py:274
  15.7 16.9 %collective-permute-start.2 = (bf16[4,320,128]{2,1,0:T(8,128)(2,1)S(1)}, bf16[4,320,128]{2,1,0:T(8,128)(2,1)S(1)}, u32[]{:S(2)}, u32[]{:S(2)}) collective-permute-start(bf16[4,320,128]{2,1,0:T(8,128)(2,1)S(1)} %merge.1), channel_id=1, source_target_pairs={{0,504},{8,16},{16,8},{24,32},{32,24},{40,48},{48,40},{56,64},{64,... | collective-permute-start | bytes 983048 | tf_op jit(solution)/shard_map/ppermute | solution.py:294
  25.7 7.1 %collective-permute-start.3 = (bf16[4,320,128]{2,1,0:T(8,128)(2,1)S(1)}, bf16[4,320,128]{2,1,0:T(8,128)(2,1)S(1)}, u32[]{:S(2)}, u32[]{:S(2)}) collective-permute-start(bf16[4,320,128]{2,1,0:T(8,128)(2,1)S(1)} %slice.3), channel_id=1, source_target_pairs={{0,8},{8,0},{16,24},{24,16},{32,40},{40,32},{48,56},{56,48},{64,72... | collective-permute-start | bytes 983048 | tf_op jit(solution)/shard_map/ppermute | solution.py:309

commit v3 on v2

--- a/solution.py
+++ b/solution.py
@@ -11,6 +11,7 @@
 WIDTH = 128
 DEV = 8
 QUAD = 4 * WIDTH
+ORDER = [4, 3, 2, 1, 0, 7, 6, 5]
 
 vertical_scale = 8.0
 
@@ -39,7 +40,7 @@
 
 
 def lift_kernel(per, blocks, pairs_hbm, count_hbm, level_hbm, ens_hbm, control_hbm, loc_hbm,
-                own_ref, band_ref, ens_ref, live_ref, pay1_ref,
+                own_ref, band_ref, ens_ref, live_ref, pay1_ref, pay3_ref,
                 pairs_ref, count_ref, level_ref, control_ref, loc_ref, vert, sems):
     members, slots, levels, columns = ens_ref.shape
     group = WIDTH // levels
@@ -128,8 +129,15 @@
     def first():
         for b in range(DEV):
             pay1_ref[b] = own_ref[:, block(b)]
+        for q in range(2, 5):
+            start = QUAD if q == 4 else 0
+            c = dot(own_ref[:, start:], band_ref[start:, q * QUAD:(q + 1) * QUAD]).astype(BF16)
+            for e in range(4):
+                pay3_ref[4 * (q - 2) + e] = c[:, block(e)]
 
     def second():
+        for b in range(DEV):
+            pay3_ref[b] = own_ref[:, block(b)]
         near = dot(own_ref[...], band_ref[:, 3 * QUAD:4 * QUAD]).astype(BF16)
         far = dot(own_ref[:, QUAD:], band_ref[QUAD:, 4 * QUAD:]).astype(BF16)
         for e in range(4):
@@ -139,30 +147,14 @@
     by_core(first, second)
 
 
-def reach_kernel(own_ref, band_ref, pay3_ref, mrg_ref):
+def merge_kernel(own_ref, band_ref, r3_ref, out_ref):
     def first():
-        for q in range(2, 5):
-            start = QUAD if q == 4 else 0
-            c = dot(own_ref[:, start:], band_ref[start:, q * QUAD:(q + 1) * QUAD]).astype(BF16)
-            for e in range(4):
-                pay3_ref[4 * (q - 2) + e] = c[:, block(e)]
+        out_ref[...] = r3_ref[:4]
 
     def second():
         c = dot(own_ref[...], band_ref[:, 2 * QUAD:3 * QUAD])
         for e in range(4):
-            mrg_ref[e] = c[:, block(e)]
-        for b in range(DEV):
-            pay3_ref[b] = own_ref[:, block(b)]
-
-    by_core(first, second)
-
-
-def merge_kernel(mrg_ref, r3_ref, out_ref):
-    def first():
-        out_ref[...] = r3_ref[:4]
-
-    def second():
-        out_ref[...] = (mrg_ref[...] + r3_ref[8:].astype(F32)).astype(BF16)
+            out_ref[e] = (c[:, block(e)] + r3_ref[8 + e].astype(F32)).astype(BF16)
 
     by_core(first, second)
 
@@ -224,7 +216,7 @@
             for t in range(slots):
                 totals[t] = totals[t] + ens_ref[m, t, :, block(b)].astype(F32) * s
         for t in range(slots):
-            out_ref[b, t] = (totals[t] * live_ref[b:b + 1, :] / (members_all - 1)).astype(BF16)
+            out_ref[ORDER.index(b), t] = (totals[t] * live_ref[b:b + 1, :] / (members_all - 1)).astype(BF16)
 
 
 def params(mib):
@@ -245,16 +237,17 @@
     tie = lax.optimization_barrier
 
     args = (pair_blocks.T, col_count, level_index, ens, control, loc_blocks)
-    own, band, ens_here, live, pay1 = pl.pallas_call(
+    own, band, ens_here, live, pay1, pay3 = pl.pallas_call(
         functools.partial(lift_kernel, per, peers * blocks_dev),
         in_specs=[HBM] * 6,
-        out_specs=[VMEM] * 5,
+        out_specs=[VMEM] * 6,
         out_shape=[
             shape((rows, columns), BF16),
             shape((columns, (DEV + SPAN) * WIDTH), BF16),
             shape(ens.shape, BF16),
             shape((DEV, WIDTH), F32),
             pieces(8, BF16),
+            pieces(12, BF16),
         ],
         scratch_shapes=[
             pltpu.SMEM((2, listed), jnp.int32),
@@ -273,27 +266,8 @@
     cores = [(i, i ^ 1) for i in range(peers)]
     r1 = lax.ppermute(pay1, "grid", chips)
 
-    pay3, mrg = pl.pallas_call(
-        reach_kernel,
-        in_specs=[VMEM] * 2,
-        out_specs=[VMEM] * 2,
-        out_shape=[pieces(12, BF16), pieces(4, F32)],
-        compiler_params=params(16),
-        name="reach",
-    )(own, band)
     r3 = lax.ppermute(pay3, "grid", cores)
 
-    pay1b = pl.pallas_call(
-        merge_kernel,
-        in_specs=[VMEM] * 2,
-        out_specs=VMEM,
-        out_shape=pieces(4, BF16),
-        compiler_params=params(12),
-        name="merge",
-    )(mrg, r3)
-    r1b = lax.ppermute(pay1b, "grid", chips)
-
-    own, pay1b = tie((own, pay1b))
     acc = pl.pallas_call(
         near_kernel,
         in_specs=[VMEM] * 2,
@@ -301,11 +275,23 @@
         out_shape=shape((rows, columns), F32),
         scratch_shapes=[pltpu.VMEM((2, QUAD, QUAD), BF16)],
         compiler_params=params(16),
-        cost_estimate=pl.CostEstimate(flops=2 * 96 * rows * WIDTH * WIDTH, bytes_accessed=6 << 20, transcendentals=0),
+        cost_estimate=pl.CostEstimate(flops=20000000000, bytes_accessed=100000000, transcendentals=0),
         name="near",
     )(own, band)
 
-    r1, acc = tie((r1, acc))
+    r3, acc = tie((r3, acc))
+    pay1b = pl.pallas_call(
+        merge_kernel,
+        in_specs=[VMEM] * 3,
+        out_specs=VMEM,
+        out_shape=pieces(4, BF16),
+        compiler_params=params(12),
+        cost_estimate=pl.CostEstimate(flops=1, bytes_accessed=1, transcendentals=0),
+        name="merge",
+    )(own, band, r3)
+    r1b = lax.ppermute(pay1b, "grid", chips)
+
+    r1, pay1b = tie((r1, pay1b))
     r3b = lax.ppermute(r1[:4], "grid", cores)
 
     acc = pl.pallas_call(
@@ -315,7 +301,7 @@
         out_shape=shape((rows, columns), F32),
         scratch_shapes=[pltpu.VMEM((rows, columns), BF16)],
         compiler_params=params(16),
-        cost_estimate=pl.CostEstimate(flops=2 * 64 * rows * WIDTH * WIDTH, bytes_accessed=6 << 20, transcendentals=0),
+        cost_estimate=pl.CostEstimate(flops=4000000000, bytes_accessed=100000000, transcendentals=0),
         name="far",
     )(band, acc, r1, r3)
 
@@ -328,7 +314,7 @@
         compiler_params=params(16),
         name="mix",
     )(ens_here, band, acc, live, r1, r3, r1b, r3b)
-    parts = lax.all_to_all(terms, "mem", 0, 0, tiled=True)
+    parts = lax.all_to_all(terms, "mem", 0, 0, tiled=True, axis_index_groups=[ORDER])
     return jnp.sum(parts.astype(F32), axis=0)
 
 

time: 52.8 us -> 48.2 us (0.913)
  the two profiles are of different devices: /device:TPU:1 before, /device:TPU:16 now
where the time goes in v3:
time: 48.2 us; the launch traced here: 48 us
  starting transfers between devices  19.1 us (40%)
  blocking collectives  13.1 us (27%)
  Pallas kernels  8.06 us (17%)
  waiting for transfers between devices  6.93 us (14%)
  other arithmetic  0.67 us (1%)
    all_to_all x1, blocking collectives, per_device(): lax.all_to_all(terms, 'mem', 0, 0, tiled=True, axis_index_groups=[ORDER])  13.1 us
    ppermute x1, starting transfers between devices, per_device(): r1 = lax.ppermute(pay1, 'grid', chips)  12.2 us
    pallas_call x1, Pallas kernels, per_device(): pl.pallas_call(functools.partial(lift_kernel, per, peers * blocks_dev), i...  4.59 us
    ppermute x1, waiting for transfers between devices, per_device(): r1b = lax.ppermute(pay1b, 'grid', chips)  4.4 us
    ppermute x1, starting transfers between devices, per_device(): r1b = lax.ppermute(pay1b, 'grid', chips)  3.04 us
    ppermute x1, starting transfers between devices, per_device(): r3 = lax.ppermute(pay3, 'grid', cores)  1.92 us
    ppermute x1, starting transfers between devices, per_device(): r3b = lax.ppermute(r1[:4], 'grid', cores)  1.92 us
    ppermute x1, waiting for transfers between devices, per_device(): r3 = lax.ppermute(pay3, 'grid', cores)  1.3 us
  transfers between devices with their start and end apart: 4, of which 4 were waited for; matrix products, arithmetic and copies ran while one was open for 0% of the time, Pallas kernels for 5%

profile of v3, /device:TPU:16, one launch (start us, length us, event | category | flops | bytes accessed | tf_op | source)
XLA Modules:
  0.0 48.0 jit_solution(8394268127224542352)
XLA Ops:
  0.0 4.6 %lift.1 = (bf16[320,1024]{1,0:T(8,128)(2,1)S(1)}, bf16[1024,2560]{1,0:T(8,128)(2,1)S(1)}, bf16[10,4,32,1024]{3,2,1,0:T(8,128)(2,1)S(1)}, f32[8,128]{1,0:T(8,128)...) custom-call(s32[2,96]{1,0:T(2,128)} %bitcast.1, s32[8]{0:T(128)} %count_hbm.1, s32[32]{0:T(128)} %level_hbm.1, ...), custom_call_target="tpu_custom_call" | custom-call | tf_op jit(solution)/shard_map/lift/pallas_call | solution.py:240
  4.6 12.2 %collective-permute-start.1 = (bf16[8,320,128]{2,1,0:T(8,128)(2,1)S(1)}, bf16[8,320,128]{2,1,0:T(8,128)(2,1)S(1)}, u32[]{:S(2)}, u32[]{:S(2)}) collective-permute-start(bf16[8,320,128]{2,1,0:T(8,128)(2,1)S(1)} %get-tuple-element.19), channel_id=1, source_target_pairs={{0,504},{8,16},{16,8},{24,32},{32,24},{40,48},{48,40},{56,64},{64,... | collective-permute-start | bytes 1966088 | tf_op jit(solution)/shard_map/ppermute | solution.py:267
  16.9 1.9 %collective-permute-start = (bf16[12,320,128]{2,1,0:T(8,128)(2,1)S(1)}, bf16[12,320,128]{2,1,0:T(8,128)(2,1)S(1)}, u32[]{:S(2)}, u32[]{:S(2)}) collective-permute-start(bf16[12,320,128]{2,1,0:T(8,128)(2,1)S(1)} %get-tuple-element.16), channel_id=1, source_target_pairs={{0,8},{8,0},{16,24},{24,16},{32,40},{40,32},{48,56},{56,48},{64,72... | collective-permute-start | bytes 2949128 | tf_op jit(solution)/shard_map/ppermute | solution.py:269
  18.8 1.2 %near.1.acc_ref = f32[320,1024]{1,0:T(8,128)S(1)} custom-call(bf16[320,1024]{1,0:T(8,128)(2,1)S(1)} %get-tuple-element.17.own_ref, bf16[1024,2560]{1,0:T(8,128)(2,1)S(1)} %get-tuple-element.15.band_ref), custom_call_target="tpu_custom_call" | custom-call | flops 20000000000 | bytes 100000000 | tf_op jit(solution)/shard_map/near/pallas_call | solution.py:271
  20.0 1.3 %collective-permute-done.r3_ref = bf16[12,320,128]{2,1,0:T(8,128)(2,1)S(1)} collective-permute-done((bf16[12,320,128]{2,1,0:T(8,128)(2,1)S(1)}, bf16[12,320,128]{2,1,0:T(8,128)(2,1)S(1)}, u32[]{:S(2)}, u32[]{:S(2)}) %collective-permute-start) | collective-permute-done | bytes 983072 | tf_op jit(solution)/shard_map/ppermute | solution.py:269
  21.3 3.0 %collective-permute-start.2 = (bf16[4,320,128]{2,1,0:T(8,128)(2,1)S(1)}, bf16[4,320,128]{2,1,0:T(8,128)(2,1)S(1)}, u32[]{:S(2)}, u32[]{:S(2)}) collective-permute-start(bf16[4,320,128]{2,1,0:T(8,128)(2,1)S(1)} %merge.1), channel_id=1, source_target_pairs={{0,504},{8,16},{16,8},{24,32},{32,24},{40,48},{48,40},{56,64},{64,... | collective-permute-start | bytes 983048 | tf_op jit(solution)/shard_map/ppermute | solution.py:292
  24.4 0.7 %collective-permute-done.1.r1_ref = bf16[8,320,128]{2,1,0:T(8,128)(2,1)S(1)} collective-permute-done((bf16[8,320,128]{2,1,0:T(8,128)(2,1)S(1)}, bf16[8,320,128]{2,1,0:T(8,128)(2,1)S(1)}, u32[]{:S(2)}, u32[]{:S(2)}) %collective-permute-start.1) | collective-permute-done | bytes 655392 | tf_op jit(solution)/shard_map/ppermute | solution.py:267
  25.1 1.9 %collective-permute-start.3 = (bf16[4,320,128]{2,1,0:T(8,128)(2,1)S(1)}, bf16[4,320,128]{2,1,0:T(8,128)(2,1)S(1)}, u32[]{:S(2)}, u32[]{:S(2)}) collective-permute-start(bf16[4,320,128]{2,1,0:T(8,128)(2,1)S(1)} %slice.3), channel_id=1, source_target_pairs={{0,8},{8,0},{16,24},{24,16},{32,40},{40,32},{48,56},{56,48},{64,72... | collective-permute-start | bytes 983048 | tf_op jit(solution)/shard_map/ppermute | solution.py:295
  27.1 1.1 %far.1.acc_ref = f32[320,1024]{1,0:T(8,128)S(1)} custom-call(bf16[1024,2560]{1,0:T(8,128)(2,1)S(1)} %get-tuple-element.15.band_ref, f32[320,1024]{1,0:T(8,128)S(1)} %near.1.acc_ref, bf16[8,320,128]{2,1,0:T(8,128)(2,1)S(1)} %collective-permute-done.1.r1_ref, bf16[12,320,128]{2,1,0:T(8,128)(2,1)S(1)} %collective-permute-done.r3_ref), custom_call_target="tpu_custom_call" | custom-call | flops 4000000000 | bytes 100000000 | tf_op jit(solution)/shard_map/far/pallas_call | solution.py:297
  28.1 0.5 %collective-permute-done.3.r3b_ref = bf16[4,320,128]{2,1,0:T(8,128)(2,1)S(1)} collective-permute-done((bf16[4,320,128]{2,1,0:T(8,128)(2,1)S(1)}, bf16[4,320,128]{2,1,0:T(8,128)(2,1)S(1)}, u32[]{:S(2)}, u32[]{:S(2)}) %collective-permute-start.3) | collective-permute-done | bytes 327712 | tf_op jit(solution)/shard_map/ppermute | solution.py:295
  28.7 4.4 %collective-permute-done.2.r1b_ref = bf16[4,320,128]{2,1,0:T(8,128)(2,1)S(1)} collective-permute-done((bf16[4,320,128]{2,1,0:T(8,128)(2,1)S(1)}, bf16[4,320,128]{2,1,0:T(8,128)(2,1)S(1)}, u32[]{:S(2)}, u32[]{:S(2)}) %collective-permute-start.2) | collective-permute-done | bytes 327712 | tf_op jit(solution)/shard_map/ppermute | solution.py:292
  33.1 1.1 %mix.1 = bf16[8,4,32,128]{3,2,1,0:T(8,128)(2,1)S(1)} custom-call(bf16[10,4,32,1024]{3,2,1,0:T(8,128)(2,1)S(1)} %get-tuple-element.14.ens_ref, bf16[1024,2560]{1,0:T(8,128)(2,1)S(1)} %get-tuple-element.15.band_ref, f32[320,1024]{1,0:T(8,128)S(1)} %far.1.acc_ref, f32[8,128]{1,0:T(8,128)S(1)} %get-tuple-element.22.live_ref, ...), custom_call_target="tpu_custom_call" | custom-call | tf_op jit(solution)/shard_map/mix/pallas_call | solution.py:308
  34.2 13.1 %all_to_all.5 = bf16[8,4,32,128]{3,2,1,0:T(8,128)(2,1)S(1)} all-to-all(bf16[8,4,32,128]{3,2,1,0:T(8,128)(2,1)S(1)} %mix.1), channel_id=1, replica_groups={{4,3,2,1,0,7,6,5},{12,11,10,9,8,15,14,13},{20,19,18,17,16,23,22,21},{28..., dimensions={0} | all-to-all | bytes 524288 | tf_op jit(solution)/shard_map/all_to_all | solution.py:317
  47.3 0.7 %convert_reduce_fusion = f32[4,32,128]{2,1,0:T(8,128)} fusion(bf16[8,4,32,128]{3,2,1,0:T(8,128)(2,1)S(1)} %all_to_all.5), kind=kLoop, calls=%fused_computation | loop fusion | flops 245760 | bytes 327680 | tf_op jit(solution)/shard_map/reduce_sum | solution.py:318
  (2 shorter events, 0.0 us)
Async XLA Ops:
  4.6 20.5 %collective-permute-start.1 = (bf16[8,320,128]{2,1,0:T(8,128)(2,1)S(1)}, bf16[8,320,128]{2,1,0:T(8,128)(2,1)S(1)}, u32[]{:S(2)}, u32[]{:S(2)}) collective-permute-start(bf16[8,320,128]{2,1,0:T(8,128)(2,1)S(1)} %get-tuple-element.19), channel_id=1, source_target_pairs={{0,504},{8,16},{16,8},{24,32},{32,24},{40,48},{48,40},{56,64},{64,... | collective-permute-start | bytes 1966088 | tf_op jit(solution)/shard_map/ppermute | solution.py:267
  16.9 4.5 %collective-permute-start = (bf16[12,320,128]{2,1,0:T(8,128)(2,1)S(1)}, bf16[12,320,128]{2,1,0:T(8,128)(2,1)S(1)}, u32[]{:S(2)}, u32[]{:S(2)}) collective-permute-start(bf16[12,320,128]{2,1,0:T(8,128)(2,1)S(1)} %get-tuple-element.16), channel_id=1, source_target_pairs={{0,8},{8,0},{16,24},{24,16},{32,40},{40,32},{48,56},{56,48},{64,72... | collective-permute-start | bytes 2949128 | tf_op jit(solution)/shard_map/ppermute | solution.py:269
  21.3 11.7 %collective-permute-start.2 = (bf16[4,320,128]{2,1,0:T(8,128)(2,1)S(1)}, bf16[4,320,128]{2,1,0:T(8,128)(2,1)S(1)}, u32[]{:S(2)}, u32[]{:S(2)}) collective-permute-start(bf16[4,320,128]{2,1,0:T(8,128)(2,1)S(1)} %merge.1), channel_id=1, source_target_pairs={{0,504},{8,16},{16,8},{24,32},{32,24},{40,48},{48,40},{56,64},{64,... | collective-permute-start | bytes 983048 | tf_op jit(solution)/shard_map/ppermute | solution.py:292
  25.1 3.5 %collective-permute-start.3 = (bf16[4,320,128]{2,1,0:T(8,128)(2,1)S(1)}, bf16[4,320,128]{2,1,0:T(8,128)(2,1)S(1)}, u32[]{:S(2)}, u32[]{:S(2)}) collective-permute-start(bf16[4,320,128]{2,1,0:T(8,128)(2,1)S(1)} %slice.3), channel_id=1, source_target_pairs={{0,8},{8,0},{16,24},{24,16},{32,40},{40,32},{48,56},{56,48},{64,72... | collective-permute-start | bytes 983048 | tf_op jit(solution)/shard_map/ppermute | solution.py:295

commit v4 on v3

--- a/solution.py
+++ b/solution.py
@@ -11,7 +11,7 @@
 WIDTH = 128
 DEV = 8
 QUAD = 4 * WIDTH
-ORDER = [4, 3, 2, 1, 0, 7, 6, 5]
+ORDER = [4, 5, 3, 6, 2, 7, 1, 0]
 
 vertical_scale = 8.0
 
@@ -186,29 +186,27 @@
     by_core(first, second)
     out_ref[...] = acc_ref[...] + dot_t(far[...], band_ref[:, 2 * QUAD:4 * QUAD])
 
-
-def mix_kernel(members_all, ens_ref, band_ref, acc_ref, live_ref, r1_ref, r3_ref, r1b_ref, r3b_ref, out_ref,
-               far, spread):
+    def first():
+        for b in range(4, DEV):
+            out_ref[:, block(b)] += r1_ref[b].astype(F32)
+
+    def second():
+        for b in range(DEV):
+            out_ref[:, block(b)] += r3_ref[b].astype(F32)
+
+    by_core(first, second)
+
+
+def mix_kernel(members_all, ens_ref, band_ref, acc_ref, live_ref, r1b_ref, r3b_ref, out_ref, far, spread):
     members, slots, levels, columns = ens_ref.shape
 
-    def first():
+    def take(lifted_ref, came_ref):
         for e in range(4):
-            far[:, block(e)] = r3b_ref[e]
-        for b in range(DEV):
-            came = r1b_ref[b] if b < 4 else r1_ref[b]
-            spread[:, block(b)] = acc_ref[:, block(b)] + came.astype(F32)
-
-    def second():
-        for e in range(4):
-            far[:, block(e)] = r1b_ref[e]
-        for b in range(DEV):
-            came = r3_ref[b].astype(F32)
-            if b < 4:
-                came = came + r3b_ref[b].astype(F32)
-            spread[:, block(b)] = acc_ref[:, block(b)] + came
-
-    by_core(first, second)
-    spread[:, QUAD:] += dot_t(far[...], band_ref[QUAD:, 4 * QUAD:])
+            far[:, block(e)] = lifted_ref[e]
+            spread[:, block(e)] = acc_ref[:, block(e)] + came_ref[e].astype(F32)
+
+    by_core(lambda: take(r3b_ref, r1b_ref), lambda: take(r1b_ref, r3b_ref))
+    spread[:, QUAD:] = acc_ref[:, QUAD:] + dot_t(far[...], band_ref[QUAD:, 4 * QUAD:])
     for b in range(DEV):
         totals = [jnp.zeros((levels, WIDTH), F32) for _ in range(slots)]
         for m in range(members):
@@ -307,13 +305,13 @@
 
     terms = pl.pallas_call(
         functools.partial(mix_kernel, members_all),
-        in_specs=[VMEM] * 8,
+        in_specs=[VMEM] * 6,
         out_specs=VMEM,
         out_shape=shape((DEV, slots, levels, WIDTH), BF16),
         scratch_shapes=[pltpu.VMEM((rows, QUAD), BF16), pltpu.VMEM((rows, columns), F32)],
         compiler_params=params(16),
         name="mix",
-    )(ens_here, band, acc, live, r1, r3, r1b, r3b)
+    )(ens_here, band, acc, live, r1b, r3b)
     parts = lax.all_to_all(terms, "mem", 0, 0, tiled=True, axis_index_groups=[ORDER])
     return jnp.sum(parts.astype(F32), axis=0)
 

time: 48.2 us -> 48 us (level)
  no operation moved by 1% of the time
where the time goes in v4:
time: 48 us; the launch traced here: 47.6 us
  starting transfers between devices  19.1 us (40%)
  blocking collectives  12.8 us (27%)
  Pallas kernels  8.12 us (17%)
  waiting for transfers between devices  6.83 us (14%)
  other arithmetic  0.67 us (1%)
    all_to_all x1, blocking collectives, per_device(): lax.all_to_all(terms, 'mem', 0, 0, tiled=True, axis_index_groups=[ORDER])  12.8 us
    ppermute x1, starting transfers between devices, per_device(): r1 = lax.ppermute(pay1, 'grid', chips)  12.2 us
    pallas_call x1, Pallas kernels, per_device(): pl.pallas_call(functools.partial(lift_kernel, per, peers * blocks_dev), i...  4.59 us
    ppermute x1, waiting for transfers between devices, per_device(): r1b = lax.ppermute(pay1b, 'grid', chips)  4.4 us
    ppermute x1, starting transfers between devices, per_device(): r1b = lax.ppermute(pay1b, 'grid', chips)  3.04 us
    ppermute x1, starting transfers between devices, per_device(): r3 = lax.ppermute(pay3, 'grid', cores)  1.92 us
    ppermute x1, starting transfers between devices, per_device(): r3b = lax.ppermute(r1[:4], 'grid', cores)  1.92 us
    ppermute x1, waiting for transfers between devices, per_device(): r3 = lax.ppermute(pay3, 'grid', cores)  1.3 us
  transfers between devices with their start and end apart: 4, of which 4 were waited for; matrix products, arithmetic and copies ran while one was open for 0% of the time, Pallas kernels for 5%

profile of v4, /device:TPU:16, one launch (start us, length us, event | category | flops | bytes accessed | tf_op | source)
XLA Modules:
  0.0 47.6 jit_solution(1884159571444658933)
XLA Ops:
  0.0 4.6 %lift.1 = (bf16[320,1024]{1,0:T(8,128)(2,1)S(1)}, bf16[1024,2560]{1,0:T(8,128)(2,1)S(1)}, bf16[10,4,32,1024]{3,2,1,0:T(8,128)(2,1)S(1)}, f32[8,128]{1,0:T(8,128)...) custom-call(s32[2,96]{1,0:T(2,128)} %bitcast.1, s32[8]{0:T(128)} %count_hbm.1, s32[32]{0:T(128)} %level_hbm.1, ...), custom_call_target="tpu_custom_call" | custom-call | tf_op jit(solution)/shard_map/lift/pallas_call | solution.py:238
  4.6 12.2 %collective-permute-start.1 = (bf16[8,320,128]{2,1,0:T(8,128)(2,1)S(1)}, bf16[8,320,128]{2,1,0:T(8,128)(2,1)S(1)}, u32[]{:S(2)}, u32[]{:S(2)}) collective-permute-start(bf16[8,320,128]{2,1,0:T(8,128)(2,1)S(1)} %get-tuple-element.19), channel_id=1, source_target_pairs={{0,504},{8,16},{16,8},{24,32},{32,24},{40,48},{48,40},{56,64},{64,... | collective-permute-start | bytes 1966088 | tf_op jit(solution)/shard_map/ppermute | solution.py:265
  16.9 1.9 %collective-permute-start = (bf16[12,320,128]{2,1,0:T(8,128)(2,1)S(1)}, bf16[12,320,128]{2,1,0:T(8,128)(2,1)S(1)}, u32[]{:S(2)}, u32[]{:S(2)}) collective-permute-start(bf16[12,320,128]{2,1,0:T(8,128)(2,1)S(1)} %get-tuple-element.16), channel_id=1, source_target_pairs={{0,8},{8,0},{16,24},{24,16},{32,40},{40,32},{48,56},{56,48},{64,72... | collective-permute-start | bytes 2949128 | tf_op jit(solution)/shard_map/ppermute | solution.py:267
  18.8 1.2 %near.1.acc_ref = f32[320,1024]{1,0:T(8,128)S(1)} custom-call(bf16[320,1024]{1,0:T(8,128)(2,1)S(1)} %get-tuple-element.17.own_ref, bf16[1024,2560]{1,0:T(8,128)(2,1)S(1)} %get-tuple-element.15.band_ref), custom_call_target="tpu_custom_call" | custom-call | flops 20000000000 | bytes 100000000 | tf_op jit(solution)/shard_map/near/pallas_call | solution.py:269
  20.0 1.3 %collective-permute-done.r3_ref = bf16[12,320,128]{2,1,0:T(8,128)(2,1)S(1)} collective-permute-done((bf16[12,320,128]{2,1,0:T(8,128)(2,1)S(1)}, bf16[12,320,128]{2,1,0:T(8,128)(2,1)S(1)}, u32[]{:S(2)}, u32[]{:S(2)}) %collective-permute-start) | collective-permute-done | bytes 983072 | tf_op jit(solution)/shard_map/ppermute | solution.py:267
  21.3 3.0 %collective-permute-start.2 = (bf16[4,320,128]{2,1,0:T(8,128)(2,1)S(1)}, bf16[4,320,128]{2,1,0:T(8,128)(2,1)S(1)}, u32[]{:S(2)}, u32[]{:S(2)}) collective-permute-start(bf16[4,320,128]{2,1,0:T(8,128)(2,1)S(1)} %merge.1), channel_id=1, source_target_pairs={{0,504},{8,16},{16,8},{24,32},{32,24},{40,48},{48,40},{56,64},{64,... | collective-permute-start | bytes 983048 | tf_op jit(solution)/shard_map/ppermute | solution.py:290
  24.4 0.7 %collective-permute-done.1.r1_ref = bf16[8,320,128]{2,1,0:T(8,128)(2,1)S(1)} collective-permute-done((bf16[8,320,128]{2,1,0:T(8,128)(2,1)S(1)}, bf16[8,320,128]{2,1,0:T(8,128)(2,1)S(1)}, u32[]{:S(2)}, u32[]{:S(2)}) %collective-permute-start.1) | collective-permute-done | bytes 655392 | tf_op jit(solution)/shard_map/ppermute | solution.py:265
  25.1 1.9 %collective-permute-start.3 = (bf16[4,320,128]{2,1,0:T(8,128)(2,1)S(1)}, bf16[4,320,128]{2,1,0:T(8,128)(2,1)S(1)}, u32[]{:S(2)}, u32[]{:S(2)}) collective-permute-start(bf16[4,320,128]{2,1,0:T(8,128)(2,1)S(1)} %slice.3), channel_id=1, source_target_pairs={{0,8},{8,0},{16,24},{24,16},{32,40},{40,32},{48,56},{56,48},{64,72... | collective-permute-start | bytes 983048 | tf_op jit(solution)/shard_map/ppermute | solution.py:293
  27.1 1.2 %far.1.acc_ref = f32[320,1024]{1,0:T(8,128)S(1)} custom-call(bf16[1024,2560]{1,0:T(8,128)(2,1)S(1)} %get-tuple-element.15.band_ref, f32[320,1024]{1,0:T(8,128)S(1)} %near.1.acc_ref, bf16[8,320,128]{2,1,0:T(8,128)(2,1)S(1)} %collective-permute-done.1.r1_ref, bf16[12,320,128]{2,1,0:T(8,128)(2,1)S(1)} %collective-permute-done.r3_ref), custom_call_target="tpu_custom_call" | custom-call | flops 4000000000 | bytes 100000000 | tf_op jit(solution)/shard_map/far/pallas_call | solution.py:295
  28.2 0.4 collective-permute-done.3.r3b_ref
  28.7 4.4 %collective-permute-done.2.r1b_ref = bf16[4,320,128]{2,1,0:T(8,128)(2,1)S(1)} collective-permute-done((bf16[4,320,128]{2,1,0:T(8,128)(2,1)S(1)}, bf16[4,320,128]{2,1,0:T(8,128)(2,1)S(1)}, u32[]{:S(2)}, u32[]{:S(2)}) %collective-permute-start.2) | collective-permute-done | bytes 327712 | tf_op jit(solution)/shard_map/ppermute | solution.py:290
  33.1 1.1 %mix.1 = bf16[8,4,32,128]{3,2,1,0:T(8,128)(2,1)S(1)} custom-call(bf16[10,4,32,1024]{3,2,1,0:T(8,128)(2,1)S(1)} %get-tuple-element.14.ens_ref, bf16[1024,2560]{1,0:T(8,128)(2,1)S(1)} %get-tuple-element.15.band_ref, f32[320,1024]{1,0:T(8,128)S(1)} %far.1.acc_ref, f32[8,128]{1,0:T(8,128)S(1)} %get-tuple-element.22.live_ref, ...), custom_call_target="tpu_custom_call" | custom-call | tf_op jit(solution)/shard_map/mix/pallas_call | solution.py:306
  34.2 12.8 %all_to_all.5 = bf16[8,4,32,128]{3,2,1,0:T(8,128)(2,1)S(1)} all-to-all(bf16[8,4,32,128]{3,2,1,0:T(8,128)(2,1)S(1)} %mix.1), channel_id=1, replica_groups={{4,5,3,6,2,7,1,0},{12,13,11,14,10,15,9,8},{20,21,19,22,18,23,17,16},{28..., dimensions={0} | all-to-all | bytes 524288 | tf_op jit(solution)/shard_map/all_to_all | solution.py:315
  46.9 0.7 %convert_reduce_fusion = f32[4,32,128]{2,1,0:T(8,128)} fusion(bf16[8,4,32,128]{3,2,1,0:T(8,128)(2,1)S(1)} %all_to_all.5), kind=kLoop, calls=%fused_computation | loop fusion | flops 245760 | bytes 327680 | tf_op jit(solution)/shard_map/reduce_sum | solution.py:316
  (2 shorter events, 0.0 us)
Async XLA Ops:
  4.6 20.5 %collective-permute-start.1 = (bf16[8,320,128]{2,1,0:T(8,128)(2,1)S(1)}, bf16[8,320,128]{2,1,0:T(8,128)(2,1)S(1)}, u32[]{:S(2)}, u32[]{:S(2)}) collective-permute-start(bf16[8,320,128]{2,1,0:T(8,128)(2,1)S(1)} %get-tuple-element.19), channel_id=1, source_target_pairs={{0,504},{8,16},{16,8},{24,32},{32,24},{40,48},{48,40},{56,64},{64,... | collective-permute-start | bytes 1966088 | tf_op jit(solution)/shard_map/ppermute | solution.py:265
  16.9 4.5 %collective-permute-start = (bf16[12,320,128]{2,1,0:T(8,128)(2,1)S(1)}, bf16[12,320,128]{2,1,0:T(8,128)(2,1)S(1)}, u32[]{:S(2)}, u32[]{:S(2)}) collective-permute-start(bf16[12,320,128]{2,1,0:T(8,128)(2,1)S(1)} %get-tuple-element.16), channel_id=1, source_target_pairs={{0,8},{8,0},{16,24},{24,16},{32,40},{40,32},{48,56},{56,48},{64,72... | collective-permute-start | bytes 2949128 | tf_op jit(solution)/shard_map/ppermute | solution.py:267
  21.3 11.7 %collective-permute-start.2 = (bf16[4,320,128]{2,1,0:T(8,128)(2,1)S(1)}, bf16[4,320,128]{2,1,0:T(8,128)(2,1)S(1)}, u32[]{:S(2)}, u32[]{:S(2)}) collective-permute-start(bf16[4,320,128]{2,1,0:T(8,128)(2,1)S(1)} %merge.1), channel_id=1, source_target_pairs={{0,504},{8,16},{16,8},{24,32},{32,24},{40,48},{48,40},{56,64},{64,... | collective-permute-start | bytes 983048 | tf_op jit(solution)/shard_map/ppermute | solution.py:290
  25.1 3.5 %collective-permute-start.3 = (bf16[4,320,128]{2,1,0:T(8,128)(2,1)S(1)}, bf16[4,320,128]{2,1,0:T(8,128)(2,1)S(1)}, u32[]{:S(2)}, u32[]{:S(2)}) collective-permute-start(bf16[4,320,128]{2,1,0:T(8,128)(2,1)S(1)} %slice.3), channel_id=1, source_target_pairs={{0,8},{8,0},{16,24},{24,16},{32,40},{40,32},{48,56},{56,48},{64,72... | collective-permute-start | bytes 983048 | tf_op jit(solution)/shard_map/ppermute | solution.py:293

commit v5 on v4

--- a/solution.py
+++ b/solution.py
@@ -102,6 +102,7 @@
         n = count * levels
         vh = vert[0, :n, :n]
         vl = vert[1, :n, :n]
+        vv = jnp.concatenate([vh, vh], axis=1)
         for c in range(0, columns, 2 * WIDTH):
             cols = slice(c, c + 2 * WIDTH)
             rows = []
@@ -113,7 +114,8 @@
             w = jnp.concatenate(rows, axis=0)
             high = w.astype(BF16)
             low = (w - high.astype(F32)).astype(BF16)
-            own_ref[m0 * levels:m0 * levels + n, cols] = (dot(vh, low) + dot(vl, high) + dot(vh, high)).astype(BF16)
+            both = jnp.concatenate([high, low], axis=0)
+            own_ref[m0 * levels:m0 * levels + n, cols] = (dot(vl, high) + dot(vv, both)).astype(BF16)
 
     for i in range(DEV):
         if i % 2 == 0:

time: 48 us -> 47.9 us (level)
  no operation moved by 1% of the time
where the time goes in v5:
time: 47.9 us; the launch traced here: 47.6 us
  starting transfers between devices  19.1 us (40%)
  blocking collectives  12.8 us (27%)
  Pallas kernels  8.07 us (17%)
  waiting for transfers between devices  6.83 us (14%)
  other arithmetic  0.67 us (1%)
    all_to_all x1, blocking collectives, per_device(): lax.all_to_all(terms, 'mem', 0, 0, tiled=True, axis_index_groups=[ORDER])  12.8 us
    ppermute x1, starting transfers between devices, per_device(): r1 = lax.ppermute(pay1, 'grid', chips)  12.2 us
    pallas_call x1, Pallas kernels, per_device(): pl.pallas_call(functools.partial(lift_kernel, per, peers * blocks_dev), i...  4.55 us
    ppermute x1, waiting for transfers between devices, per_device(): r1b = lax.ppermute(pay1b, 'grid', chips)  4.4 us
    ppermute x1, starting transfers between devices, per_device(): r1b = lax.ppermute(pay1b, 'grid', chips)  3.04 us
    ppermute x1, starting transfers between devices, per_device(): r3b = lax.ppermute(r1[:4], 'grid', cores)  1.92 us
    ppermute x1, starting transfers between devices, per_device(): r3 = lax.ppermute(pay3, 'grid', cores)  1.92 us
    ppermute x1, waiting for transfers between devices, per_device(): r3 = lax.ppermute(pay3, 'grid', cores)  1.3 us
  transfers between devices with their start and end apart: 4, of which 4 were waited for; matrix products, arithmetic and copies ran while one was open for 0% of the time, Pallas kernels for 5%

profile of v5, /device:TPU:16, one launch (start us, length us, event | category | flops | bytes accessed | tf_op | source)
XLA Modules:
  0.0 47.6 jit_solution(12558599853283329535)
XLA Ops:
  0.0 4.5 %lift.1 = (bf16[320,1024]{1,0:T(8,128)(2,1)S(1)}, bf16[1024,2560]{1,0:T(8,128)(2,1)S(1)}, bf16[10,4,32,1024]{3,2,1,0:T(8,128)(2,1)S(1)}, f32[8,128]{1,0:T(8,128)...) custom-call(s32[2,96]{1,0:T(2,128)} %bitcast.1, s32[8]{0:T(128)} %count_hbm.1, s32[32]{0:T(128)} %level_hbm.1, ...), custom_call_target="tpu_custom_call" | custom-call | tf_op jit(solution)/shard_map/lift/pallas_call | solution.py:240
  4.6 12.2 %collective-permute-start.1 = (bf16[8,320,128]{2,1,0:T(8,128)(2,1)S(1)}, bf16[8,320,128]{2,1,0:T(8,128)(2,1)S(1)}, u32[]{:S(2)}, u32[]{:S(2)}) collective-permute-start(bf16[8,320,128]{2,1,0:T(8,128)(2,1)S(1)} %get-tuple-element.19), channel_id=1, source_target_pairs={{0,504},{8,16},{16,8},{24,32},{32,24},{40,48},{48,40},{56,64},{64,... | collective-permute-start | bytes 1966088 | tf_op jit(solution)/shard_map/ppermute | solution.py:267
  16.8 1.9 %collective-permute-start = (bf16[12,320,128]{2,1,0:T(8,128)(2,1)S(1)}, bf16[12,320,128]{2,1,0:T(8,128)(2,1)S(1)}, u32[]{:S(2)}, u32[]{:S(2)}) collective-permute-start(bf16[12,320,128]{2,1,0:T(8,128)(2,1)S(1)} %get-tuple-element.16), channel_id=1, source_target_pairs={{0,8},{8,0},{16,24},{24,16},{32,40},{40,32},{48,56},{56,48},{64,72... | collective-permute-start | bytes 2949128 | tf_op jit(solution)/shard_map/ppermute | solution.py:269
  18.7 1.2 %near.1.acc_ref = f32[320,1024]{1,0:T(8,128)S(1)} custom-call(bf16[320,1024]{1,0:T(8,128)(2,1)S(1)} %get-tuple-element.17.own_ref, bf16[1024,2560]{1,0:T(8,128)(2,1)S(1)} %get-tuple-element.15.band_ref), custom_call_target="tpu_custom_call" | custom-call | flops 20000000000 | bytes 100000000 | tf_op jit(solution)/shard_map/near/pallas_call | solution.py:271
  20.0 1.3 %collective-permute-done.r3_ref = bf16[12,320,128]{2,1,0:T(8,128)(2,1)S(1)} collective-permute-done((bf16[12,320,128]{2,1,0:T(8,128)(2,1)S(1)}, bf16[12,320,128]{2,1,0:T(8,128)(2,1)S(1)}, u32[]{:S(2)}, u32[]{:S(2)}) %collective-permute-start) | collective-permute-done | bytes 983072 | tf_op jit(solution)/shard_map/ppermute | solution.py:269
  21.3 3.0 %collective-permute-start.2 = (bf16[4,320,128]{2,1,0:T(8,128)(2,1)S(1)}, bf16[4,320,128]{2,1,0:T(8,128)(2,1)S(1)}, u32[]{:S(2)}, u32[]{:S(2)}) collective-permute-start(bf16[4,320,128]{2,1,0:T(8,128)(2,1)S(1)} %merge.1), channel_id=1, source_target_pairs={{0,504},{8,16},{16,8},{24,32},{32,24},{40,48},{48,40},{56,64},{64,... | collective-permute-start | bytes 983048 | tf_op jit(solution)/shard_map/ppermute | solution.py:292
  24.3 0.7 %collective-permute-done.1.r1_ref = bf16[8,320,128]{2,1,0:T(8,128)(2,1)S(1)} collective-permute-done((bf16[8,320,128]{2,1,0:T(8,128)(2,1)S(1)}, bf16[8,320,128]{2,1,0:T(8,128)(2,1)S(1)}, u32[]{:S(2)}, u32[]{:S(2)}) %collective-permute-start.1) | collective-permute-done | bytes 655392 | tf_op jit(solution)/shard_map/ppermute | solution.py:267
  25.1 1.9 %collective-permute-start.3 = (bf16[4,320,128]{2,1,0:T(8,128)(2,1)S(1)}, bf16[4,320,128]{2,1,0:T(8,128)(2,1)S(1)}, u32[]{:S(2)}, u32[]{:S(2)}) collective-permute-start(bf16[4,320,128]{2,1,0:T(8,128)(2,1)S(1)} %slice.3), channel_id=1, source_target_pairs={{0,8},{8,0},{16,24},{24,16},{32,40},{40,32},{48,56},{56,48},{64,72... | collective-permute-start | bytes 983048 | tf_op jit(solution)/shard_map/ppermute | solution.py:295
  27.0 1.2 %far.1.acc_ref = f32[320,1024]{1,0:T(8,128)S(1)} custom-call(bf16[1024,2560]{1,0:T(8,128)(2,1)S(1)} %get-tuple-element.15.band_ref, f32[320,1024]{1,0:T(8,128)S(1)} %near.1.acc_ref, bf16[8,320,128]{2,1,0:T(8,128)(2,1)S(1)} %collective-permute-done.1.r1_ref, bf16[12,320,128]{2,1,0:T(8,128)(2,1)S(1)} %collective-permute-done.r3_ref), custom_call_target="tpu_custom_call" | custom-call | flops 4000000000 | bytes 100000000 | tf_op jit(solution)/shard_map/far/pallas_call | solution.py:297
  28.2 0.4 collective-permute-done.3.r3b_ref
  28.6 4.4 %collective-permute-done.2.r1b_ref = bf16[4,320,128]{2,1,0:T(8,128)(2,1)S(1)} collective-permute-done((bf16[4,320,128]{2,1,0:T(8,128)(2,1)S(1)}, bf16[4,320,128]{2,1,0:T(8,128)(2,1)S(1)}, u32[]{:S(2)}, u32[]{:S(2)}) %collective-permute-start.2) | collective-permute-done | bytes 327712 | tf_op jit(solution)/shard_map/ppermute | solution.py:292
  33.0 1.1 %mix.1 = bf16[8,4,32,128]{3,2,1,0:T(8,128)(2,1)S(1)} custom-call(bf16[10,4,32,1024]{3,2,1,0:T(8,128)(2,1)S(1)} %get-tuple-element.14.ens_ref, bf16[1024,2560]{1,0:T(8,128)(2,1)S(1)} %get-tuple-element.15.band_ref, f32[320,1024]{1,0:T(8,128)S(1)} %far.1.acc_ref, f32[8,128]{1,0:T(8,128)S(1)} %get-tuple-element.22.live_ref, ...), custom_call_target="tpu_custom_call" | custom-call | tf_op jit(solution)/shard_map/mix/pallas_call | solution.py:308
  34.1 12.8 %all_to_all.5 = bf16[8,4,32,128]{3,2,1,0:T(8,128)(2,1)S(1)} all-to-all(bf16[8,4,32,128]{3,2,1,0:T(8,128)(2,1)S(1)} %mix.1), channel_id=1, replica_groups={{4,5,3,6,2,7,1,0},{12,13,11,14,10,15,9,8},{20,21,19,22,18,23,17,16},{28..., dimensions={0} | all-to-all | bytes 524288 | tf_op jit(solution)/shard_map/all_to_all | solution.py:317
  46.9 0.7 %convert_reduce_fusion = f32[4,32,128]{2,1,0:T(8,128)} fusion(bf16[8,4,32,128]{3,2,1,0:T(8,128)(2,1)S(1)} %all_to_all.5), kind=kLoop, calls=%fused_computation | loop fusion | flops 245760 | bytes 327680 | tf_op jit(solution)/shard_map/reduce_sum | solution.py:318
  (2 shorter events, 0.0 us)
Async XLA Ops:
  4.6 20.5 %collective-permute-start.1 = (bf16[8,320,128]{2,1,0:T(8,128)(2,1)S(1)}, bf16[8,320,128]{2,1,0:T(8,128)(2,1)S(1)}, u32[]{:S(2)}, u32[]{:S(2)}) collective-permute-start(bf16[8,320,128]{2,1,0:T(8,128)(2,1)S(1)} %get-tuple-element.19), channel_id=1, source_target_pairs={{0,504},{8,16},{16,8},{24,32},{32,24},{40,48},{48,40},{56,64},{64,... | collective-permute-start | bytes 1966088 | tf_op jit(solution)/shard_map/ppermute | solution.py:267
  16.8 4.5 %collective-permute-start = (bf16[12,320,128]{2,1,0:T(8,128)(2,1)S(1)}, bf16[12,320,128]{2,1,0:T(8,128)(2,1)S(1)}, u32[]{:S(2)}, u32[]{:S(2)}) collective-permute-start(bf16[12,320,128]{2,1,0:T(8,128)(2,1)S(1)} %get-tuple-element.16), channel_id=1, source_target_pairs={{0,8},{8,0},{16,24},{24,16},{32,40},{40,32},{48,56},{56,48},{64,72... | collective-permute-start | bytes 2949128 | tf_op jit(solution)/shard_map/ppermute | solution.py:269
  21.3 11.7 %collective-permute-start.2 = (bf16[4,320,128]{2,1,0:T(8,128)(2,1)S(1)}, bf16[4,320,128]{2,1,0:T(8,128)(2,1)S(1)}, u32[]{:S(2)}, u32[]{:S(2)}) collective-permute-start(bf16[4,320,128]{2,1,0:T(8,128)(2,1)S(1)} %merge.1), channel_id=1, source_target_pairs={{0,504},{8,16},{16,8},{24,32},{32,24},{40,48},{48,40},{56,64},{64,... | collective-permute-start | bytes 983048 | tf_op jit(solution)/shard_map/ppermute | solution.py:292
  25.1 3.5 %collective-permute-start.3 = (bf16[4,320,128]{2,1,0:T(8,128)(2,1)S(1)}, bf16[4,320,128]{2,1,0:T(8,128)(2,1)S(1)}, u32[]{:S(2)}, u32[]{:S(2)}) collective-permute-start(bf16[4,320,128]{2,1,0:T(8,128)(2,1)S(1)} %slice.3), channel_id=1, source_target_pairs={{0,8},{8,0},{16,24},{24,16},{32,40},{40,32},{48,56},{56,48},{64,72... | collective-permute-start | bytes 983048 | tf_op jit(solution)/shard_map/ppermute | solution.py:295
